TPU v7x, 32 devices: a whole 2x2x4 slice. The times are simulated.
32 devices in a mesh: sec: 2 (over core), dom: 16 (over z, y, x).
Axes of the slice: x: 2, y: 2, z: 4, core: 2. Of those that a mesh axis runs over, the one named last changes fastest.
Arguments:
- state: float32 [3, 8, 262144], P(None, None, ('sec', 'dom')), may hold values from -6 to 6
- send_rows: int32 [524288], P(('sec', 'dom')), may hold values from 0 to 8191, as said below
- intersection_source: int32 [524288], P(('sec', 'dom')), may hold values from 0 to 16383, as said below
- intersection_weight: float32 [524288], P(('sec', 'dom')), may hold values from 0.1 to 1
- couple_rate: float32 [2, 3], P('sec'), may hold values from 0.2 to 0.8
- atm_metric: float32 [2, 131072], P(None, 'dom'), may hold values from 0.5 to 2
- wave_speed: float32 [8], replicated, may hold values from 0.5 to 2
- ocean_adjacent: int32 [6, 131072], P(None, 'dom'), may hold values from 0 to 9215, as said below
- ocean_edges: int32 [2, 8192], P(None, 'dom'), may hold values from 0 to 8191, as said below
- ocean_kappa: float32 [131072], P('dom'), may hold values from 0.02 to 0.15
Outputs:
- new_state: float32 [3, 8, 262144], P(None, None, ('sec', 'dom'))
Inputs may be any that keep to these rules, and one draw needn't show every extreme that they name: `send_rows`: the ocean's band runs across the atmosphere's, so every block intersects every block of the other section. Within a block, cut the rows into 16 strips of 512 rows by position across the band; the 1024 slots for peer p hold the rows of strips p, p + 1, ... (modulo 16), 2 strips in all, in an order drawn from the seed; so every row fills exactly 2 slots. `intersection_source`: in each block a permutation of all 16384 received slots; the entries 2 * r .. 2 * r + 1 belong to row r. `ocean_adjacent`: each cell's neighbours on a hexagonal grid in its block's own row order; values from 8192 on name rim slots (first the cells of the previous block's last column, then those of the next block's first column, by position across the band); a cell at the band's edge names itself for a missing neighbour. `ocean_edges`: ordered by position across the band.
All inputs are finite; a program needn't handle non-finite values.
Results may differ from a plain program's by a relative error of at most 0.0001.
Values sent between devices are 32-bit elements; how exact they have to be, the bound alone decides.
A program may use at most 128 MiB of HBM per device.

v0:
```python
import functools
import jax
import jax.numpy as jnp
import numpy as np
from jax import lax
from jax.experimental import pallas as pl
from jax.experimental.pallas import tpu as pltpu
from jax.sharding import PartitionSpec as P

TIME_STEP = 0.05
LANES = 128
VMEM = pl.BlockSpec(memory_space=pltpu.VMEM)
SMEM = pl.BlockSpec(memory_space=pltpu.SMEM)
PARAMS = dict(vmem_limit_bytes=48 << 20)


def gll_derivative():
    nodes = np.array([-1.0, -1.0 / np.sqrt(5.0), 1.0 / np.sqrt(5.0), 1.0])
    barycentric = np.array(
        [1.0 / np.prod([nodes[i] - nodes[j] for j in range(4) if j != i]) for i in range(4)]
    )
    matrix = np.zeros((4, 4))
    for i in range(4):
        for j in range(4):
            if i != j:
                matrix[i, j] = barycentric[j] / barycentric[i] / (nodes[i] - nodes[j])
        matrix[i, i] = -np.sum(matrix[i])
    return matrix


DERIVATIVE = gll_derivative()


def two_terms(table):
    high = table.astype(jnp.bfloat16)
    low = (table - high.astype(jnp.float32)).astype(jnp.bfloat16)
    return jnp.concatenate([high, low], axis=1)


def pick(terms, depth, index):
    low = jnp.broadcast_to(index & (LANES - 1), (LANES, index.shape[1]))
    hot = (lax.broadcasted_iota(jnp.int32, low.shape, 0) == low).astype(jnp.float32).astype(jnp.bfloat16)
    found = jnp.dot(terms, jnp.concatenate([hot, hot], axis=0), preferred_element_type=jnp.float32)
    high = jnp.broadcast_to(index >> 7, (depth, index.shape[1]))
    own = lax.broadcasted_iota(jnp.int32, high.shape, 0) == high
    return [
        jnp.sum(jnp.where(own, found[f * depth : (f + 1) * depth], 0.0), axis=0, keepdims=True)
        for f in range(3)
    ]


def lane_phase(shape):
    return lax.broadcasted_iota(jnp.int32, shape, 1) % 4


def along_second(value, phase):
    width = value.shape[1]
    total = jnp.zeros_like(value)
    for shift in range(-3, 4):
        factor = jnp.zeros(value.shape, jnp.float32)
        for i in range(4):
            if 0 <= i + shift < 4:
                factor = jnp.where(phase == i, np.float32(DERIVATIVE[i, i + shift]), factor)
        moved = value if shift == 0 else pltpu.roll(value, (-shift) % width, 1)
        total = total + factor * moved
    return total


def advance(x_points, y_points, state_ref, metric_ref, speed_ref, stepped_ref):
    level = lax.broadcasted_iota(jnp.int32, (state_ref.shape[1], LANES), 0)
    speed = jnp.zeros(level.shape, jnp.float32)
    for k in range(level.shape[0]):
        speed = jnp.where(level == k, speed_ref[k], speed)

    def piece(g, _):
        def at(i, f):
            return state_ref[f, :, pl.ds(pl.multiple_of(start + i * y_points, LANES), LANES)]

        start = (g // (y_points // LANES)) * 4 * y_points + (g % (y_points // LANES)) * LANES
        phase = lane_phase((state_ref.shape[1], LANES))
        u = [at(i, 0) for i in range(4)]
        v = [at(i, 1) for i in range(4)]
        h = [at(i, 2) for i in range(4)]
        for i in range(4):
            here = pl.ds(pl.multiple_of(start + i * y_points, LANES), LANES)
            gx = metric_ref[0:1, here]
            gy = metric_ref[1:2, here]
            dx_h = sum(np.float32(DERIVATIVE[i, j]) * h[j] for j in range(4))
            dx_u = sum(np.float32(DERIVATIVE[i, j]) * u[j] for j in range(4))
            stepped_ref[0, :, here] = u[i] - TIME_STEP * (gx * dx_h)
            stepped_ref[1, :, here] = v[i] - TIME_STEP * (gy * along_second(h[i], phase))
            spread = gx * dx_u + gy * along_second(v[i], phase)
            stepped_ref[2, :, here] = h[i] - TIME_STEP * speed * spread
        return 0

    lax.fori_loop(0, x_points // 4 * (y_points // LANES), piece, 0)


def to_rows(source_ref, source_at, table_ref, table_at, count):
    def piece(c, _):
        here = pl.ds(pl.multiple_of(source_at + c * LANES, LANES), LANES)
        block = jnp.concatenate([source_ref[f, :, here] for f in range(3)], axis=0)
        there = pl.ds(pl.multiple_of(table_at + c * LANES, LANES), LANES)
        table_ref[there, : block.shape[0]] = jnp.transpose(block)
        return 0

    lax.fori_loop(0, count // LANES, piece, 0, unroll=4)


def from_rows(table_ref, at, levels):
    block = jnp.transpose(table_ref[pl.ds(pl.multiple_of(at, LANES), LANES), :])
    return [block[f * levels : (f + 1) * levels] for f in range(3)]


def pick_edges(state_ref, edges_ref, border_ref, table_ref, picked_ref):
    side = edges_ref.shape[1]
    count = 2 * side
    to_rows(state_ref, 0, table_ref, 0, state_ref.shape[2])

    def step(i, _):
        base = i * 8
        places = [[edges_ref[k, base + u] for u in range(8)] for k in range(2)]
        for k in range(2):
            for u in range(8):
                picked_ref[pl.ds(k * side + base + u, 1), :] = table_ref[pl.ds(places[k][u], 1), :]
        return 0

    lax.fori_loop(0, side // 8, step, 0)
    for c in range(count // LANES):
        block = from_rows(picked_ref, c * LANES, state_ref.shape[1])
        for f in range(3):
            border_ref[f, :, c * LANES : (c + 1) * LANES] = block[f]


def prepare_kernel(
    n, x_points, y_points, rows_ref, state_ref, edges_ref, metric_ref, speed_ref,
    in_ref, stepped_ref, west_a_ref, east_a_ref, west_o_ref, east_o_ref, ocean_ref,
    surface_ref, terms_ref, out_ref, rim_ref, table_ref, picked_ref, send_sem, recv_sem, edge_send_sem, edge_recv_sem,
):
    sec, dom = lax.axis_index("sec"), lax.axis_index("dom")
    right, left = lax.rem(dom + 1, n), lax.rem(dom + n - 1, n)
    mesh_ids = pl.DeviceIdType.MESH
    barrier = pltpu.get_barrier_semaphore()

    def greet(p, _):
        pl.semaphore_signal(barrier, inc=1, device_id=(1 - sec, p), device_id_type=mesh_ids)
        return 0

    lax.fori_loop(0, n, greet, 0)
    for side in (left, right):
        pl.semaphore_signal(barrier, inc=1, device_id=(sec, side), device_id_type=mesh_ids)

    @pl.when(sec == 0)
    def _():
        advance(x_points, y_points, state_ref, metric_ref, speed_ref, stepped_ref)

    @pl.when(sec == 1)
    def _():
        pick_edges(state_ref, edges_ref, rim_ref, table_ref, picked_ref)

    pl.semaphore_wait(barrier, n + 2)

    rows = state_ref.shape[2]
    first, last = pl.ds(0, y_points), pl.ds(rows - y_points, y_points)

    def edge(k, source, target, arrival, device):
        return pltpu.make_async_remote_copy(
            src_ref=source,
            dst_ref=target,
            send_sem=edge_send_sem.at[k],
            recv_sem=edge_recv_sem.at[arrival],
            device_id=device,
            device_id_type=mesh_ids,
        )

    rim_last, rim_first = rim_ref.at[:, :, pl.ds(y_points, y_points)], rim_ref.at[:, :, first]
    ocean_edges = [
        edge(0, rim_last, west_o_ref, 0, (1, right)),
        edge(1, rim_first, east_o_ref, 1, (1, left)),
        edge(2, rim_last, west_o_ref, 0, (0, right)),
        edge(3, rim_first, east_o_ref, 1, (0, left)),
        edge(4, state_ref, ocean_ref, 4, (0, dom)),
    ]
    atmosphere_edges = [
        edge(0, stepped_ref.at[:, :, last], west_a_ref, 2, (0, right)),
        edge(1, stepped_ref.at[:, :, first], east_a_ref, 3, (0, left)),
    ]

    @pl.when(sec == 0)
    def _():
        for each in atmosphere_edges:
            each.start()

    @pl.when(sec == 1)
    def _():
        for each in ocean_edges:
            each.start()

    depth, top = rows // LANES, state_ref.shape[1] - 1
    for h in range(depth):
        for f in range(3):
            surface_ref[f * depth + h : f * depth + h + 1, :] = state_ref[
                f, top : top + 1, h * LANES : (h + 1) * LANES
            ]
    terms_ref[...] = two_terms(surface_ref[...])
    per_peer = out_ref.shape[2]

    def copy(k):
        p = lax.rem(dom + k, n)
        return pltpu.make_async_remote_copy(
            src_ref=out_ref.at[p],
            dst_ref=in_ref.at[dom],
            send_sem=send_sem.at[k],
            recv_sem=recv_sem.at[k],
            device_id=(1 - sec, p),
            device_id_type=mesh_ids,
        )

    def start(k, _):
        p = lax.rem(dom + k, n)
        for i in range(per_peer // 2):
            place = p * per_peer + 2 * i
            index = jnp.concatenate(
                [rows_ref[pl.ds(place, 1), :], rows_ref[pl.ds(place + 1, 1), :]], axis=1
            )
            values = pick(terms_ref[...], depth, index)
            for f in range(3):
                for half in range(2):
                    out_ref[p, f, 2 * i + half : 2 * i + half + 1, :] = values[f][
                        :, half * LANES : (half + 1) * LANES
                    ]
        copy(k).start()
        return 0

    def wait(k, _):
        copy(k).wait()
        return 0

    lax.fori_loop(0, n, start, 0)
    lax.fori_loop(0, n, wait, 0)

    @pl.when(sec == 0)
    def _():
        for each in atmosphere_edges:
            each.wait()
        ocean_edges[0].wait_recv()
        ocean_edges[1].wait_recv()
        ocean_edges[4].wait_recv()

    @pl.when(sec == 1)
    def _():
        for each in ocean_edges:
            each.wait_send()
        ocean_edges[0].wait_recv()
        ocean_edges[1].wait_recv()


def deinterleave(values, offset):
    count = values.shape[0]
    i = lax.broadcasted_iota(jnp.int32, (LANES, LANES), 0)
    j = lax.broadcasted_iota(jnp.int32, (LANES, LANES), 1)
    m = lax.broadcasted_iota(jnp.int32, (count // 2, count), 0)
    q = lax.broadcasted_iota(jnp.int32, (count // 2, count), 1)
    total = jnp.zeros((count // 2, LANES), jnp.float32)
    for b in range(2):
        chosen = (i == 2 * (j - b * (LANES // 2)) + offset).astype(jnp.float32)
        packed = jnp.dot(
            values, chosen, preferred_element_type=jnp.float32, precision=lax.Precision.HIGHEST
        )
        gathered = (q == 2 * m + b).astype(jnp.float32)
        total = total + jnp.dot(
            gathered, packed, preferred_element_type=jnp.float32, precision=lax.Precision.HIGHEST
        )
    return total


def sweep_kernel(
    state_ref, west_ref, east_ref, adjacent_ref, kappa_ref, incoming_ref, source_ref, weight_ref,
    swept_ref, regrid_ref, table_ref, sum_ref, terms_ref, index_ref, share_ref,
):
    levels, rows, edge = state_ref.shape[1], state_ref.shape[2], west_ref.shape[2]
    part = swept_ref.shape[2]
    to_rows(state_ref, 0, table_ref, 0, rows)
    to_rows(west_ref, 0, table_ref, rows, edge)
    to_rows(east_ref, 0, table_ref, rows + edge, edge)

    depth = source_ref.shape[0]
    for f in range(3):
        table = incoming_ref[:, f].reshape(depth, LANES)
        terms_ref[f * depth : (f + 1) * depth, :] = two_terms(table)
    source = source_ref[...].astype(jnp.float32)
    for k in range(2):
        index_ref[:, k * LANES : (k + 1) * LANES] = (deinterleave(source, k) + 0.5).astype(jnp.int32)
        share_ref[:, k * LANES : (k + 1) * LANES] = deinterleave(weight_ref[...], k)

    steps = depth // 2
    cells = part // steps

    def step(c, _):
        values = pick(terms_ref[...], depth, index_ref[pl.ds(c, 1), :])
        for u in range(cells):
            cell = c * cells + u
            places = [adjacent_ref[c * cells + (j * part + u)] for j in range(6)]
            a = [table_ref[pl.ds(p, 1), :] for p in places]
            sum_ref[pl.ds(cell, 1), :] = ((a[0] + a[1]) + (a[2] + a[3])) + (a[4] + a[5])
        weight = share_ref[pl.ds(c, 1), :]
        whole = weight[:, :LANES] + weight[:, LANES:]
        here = pl.ds(pl.multiple_of(c * LANES, LANES), LANES)
        for f in range(3):
            product = values[f] * weight
            regrid_ref[f : f + 1, here] = (product[:, :LANES] + product[:, LANES:]) / whole
        return 0

    lax.fori_loop(0, steps, step, 0)
    first = lax.axis_index("sec") * (part // LANES)

    def finish(c, _):
        here = pl.ds(pl.multiple_of(c * LANES, LANES), LANES)
        there = pl.ds(pl.multiple_of((first + c) * LANES, LANES), LANES)
        block = from_rows(sum_ref, c * LANES, levels)
        kappa = kappa_ref[pl.ds(first + c, 1), :]
        for f in range(3):
            value = state_ref[f, :, there]
            swept_ref[f, :, here] = value + kappa * (block[f] - 6.0 * value)
        return 0

    lax.fori_loop(0, part // LANES, finish, 0, unroll=4)


def finish_kernel(
    x_points, y_points, regrid_ref, rate_ref, stepped_ref, west_ref, east_ref, own_ref, helped_ref, new_ref,
):
    atmosphere = lax.axis_index("sec") == 0
    levels = stepped_ref.shape[1]

    def couple(f, here, value):
        rate = rate_ref[0, f]
        row = lax.broadcasted_iota(jnp.int32, value.shape, 0)
        relaxed = value + rate * (regrid_ref[f : f + 1, here] - value)
        new_ref[f, :, here] = jnp.where(row == levels - 1, relaxed, value)

    @pl.when(atmosphere)
    def _():
        for f in range(3):
            for x in range(x_points):
                here = slice(x * y_points, (x + 1) * y_points)
                value = stepped_ref[f, :, here]
                if x % 4 == 3:
                    other = (
                        stepped_ref[f, :, (x + 1) * y_points : (x + 2) * y_points]
                        if x < x_points - 1
                        else east_ref[f]
                    )
                    value = (value + other) * 0.5
                elif x % 4 == 0:
                    other = stepped_ref[f, :, (x - 1) * y_points : x * y_points] if x else west_ref[f]
                    value = (value + other) * 0.5
                position = lax.broadcasted_iota(jnp.int32, value.shape, 1)
                phase = position % 4
                after = pltpu.roll(value, y_points - 1, 1)
                before = pltpu.roll(value, 1, 1)
                averaged = jnp.where(
                    (phase == 3) & (position < y_points - 1),
                    (value + after) * 0.5,
                    jnp.where((phase == 0) & (position > 0), (value + before) * 0.5, value),
                )
                couple(f, here, averaged)

    @pl.when(jnp.logical_not(atmosphere))
    def _():
        part = own_ref.shape[2]
        for f in range(3):
            couple(f, slice(0, part), helped_ref[f])
            couple(f, slice(part, 2 * part), own_ref[f])


def body(
    state, send_rows, intersection_source, intersection_weight, couple_rate, atm_metric, wave_speed,
    ocean_adjacent, ocean_edges, ocean_kappa,
):
    levels, rows = state.shape[1], state.shape[2]
    y_points = ocean_edges.shape[1]
    x_points = rows // y_points
    n = lax.axis_size("dom")
    sec = lax.axis_index("sec")
    slots = send_rows.shape[0]
    cap = slots // n
    part = rows // 2
    f32 = jnp.float32

    border = jax.ShapeDtypeStruct((3, levels, y_points), f32)
    whole = jax.ShapeDtypeStruct(state.shape, f32)
    arriving = jax.ShapeDtypeStruct((n, 3, cap // LANES, LANES), f32)
    incoming, stepped, west_a, east_a, west_o, east_o, ocean = pl.pallas_call(
        functools.partial(prepare_kernel, n, x_points, y_points),
        out_shape=[arriving, whole] + [border] * 4 + [whole],
        in_specs=[VMEM] * 2 + [SMEM, VMEM, SMEM],
        out_specs=[VMEM] * 7,
        scratch_shapes=[
            pltpu.VMEM((3 * rows // LANES, LANES), f32),
            pltpu.VMEM((3 * rows // LANES, 2 * LANES), jnp.bfloat16),
            pltpu.VMEM(arriving.shape, f32),
            pltpu.VMEM((3, levels, 2 * y_points), f32),
            pltpu.VMEM((rows, LANES), f32),
            pltpu.VMEM((2 * y_points, LANES), f32),
            pltpu.SemaphoreType.DMA((n,)),
            pltpu.SemaphoreType.DMA((n,)),
            pltpu.SemaphoreType.DMA((5,)),
            pltpu.SemaphoreType.DMA((5,)),
        ],
        compiler_params=pltpu.CompilerParams(collective_id=0, has_side_effects=True, **PARAMS),
        cost_estimate=pl.CostEstimate(
            flops=6 * rows * LANES * slots // LANES, bytes_accessed=3 * state.size * 4, transcendentals=0
        ),
        name="prepare",
    )(
        send_rows.reshape(-1, LANES),
        state,
        ocean_edges,
        atm_metric,
        wave_speed,
    )

    ocean = jnp.where(sec == 0, ocean, state)
    adjacent = lax.dynamic_slice_in_dim(ocean_adjacent, sec * part, part, 1).reshape(-1)
    swept, regrid = pl.pallas_call(
        sweep_kernel,
        out_shape=[jax.ShapeDtypeStruct((3, levels, part), f32), jax.ShapeDtypeStruct((3, rows), f32)],
        in_specs=[VMEM] * 3 + [SMEM] + [VMEM] * 4,
        out_specs=[VMEM] * 2,
        scratch_shapes=[
            pltpu.VMEM((rows + 2 * y_points, LANES), f32),
            pltpu.VMEM((part, LANES), f32),
            pltpu.VMEM((3 * slots // LANES, 2 * LANES), jnp.bfloat16),
            pltpu.VMEM((slots // LANES // 2, 2 * LANES), jnp.int32),
            pltpu.VMEM((slots // LANES // 2, 2 * LANES), f32),
        ],
        compiler_params=pltpu.CompilerParams(**PARAMS),
        name="sweep",
    )(
        ocean, west_o, east_o, adjacent, ocean_kappa.reshape(-1, LANES), incoming,
        intersection_source.reshape(-1, LANES), intersection_weight.reshape(-1, LANES),
    )
    helped = lax.ppermute(swept, "sec", [(0, 1)])

    return pl.pallas_call(
        functools.partial(finish_kernel, x_points, y_points),
        out_shape=jax.ShapeDtypeStruct(state.shape, f32),
        in_specs=[VMEM, SMEM] + [VMEM] * 5,
        out_specs=VMEM,
        compiler_params=pltpu.CompilerParams(**PARAMS),
        name="finish",
    )(regrid, couple_rate, stepped, west_a, east_a, swept, helped)


def solution(mesh):
    in_specs = (
        P(None, None, ("sec", "dom")),
        P(("sec", "dom")),
        P(("sec", "dom")),
        P(("sec", "dom")),
        P("sec", None),
        P(None, "dom"),
        P(),
        P(None, "dom"),
        P(None, "dom"),
        P("dom"),
    )
    out_specs = P(None, None, ("sec", "dom"))
    return jax.shard_map(body, mesh=mesh, in_specs=in_specs, out_specs=out_specs, check_vma=False)
```

profile of v0, /device:TPU:1, one launch (start us, length us, event | category | flops | bytes accessed | tf_op | source)
XLA Modules:
  0.0 53.2 jit_solution(13047977903814825197)
XLA Ops:
  0.0 0.0 copy-start
  0.0 0.9 %copy-done = s32[6,8192]{1,0:T(8,128)S(1)} copy-done((s32[6,8192]{1,0:T(8,128)S(1)}, s32[6,8192]{1,0:T(8,128)}, u32[]{:S(2)}) %copy-start) | copy-done | bytes 196632
  1.0 0.0 copy-start.7
  1.0 0.0 copy-start.8
  1.0 0.0 copy-start.9
  1.0 0.1 reshape.16.adjacent_ref
  1.1 0.0 copy-start.10
  1.1 0.7 %copy-done.7 = s32[16384]{0:T(1024)S(1)} copy-done((s32[16384]{0:T(1024)S(1)}, s32[16384]{0:T(1024)}, u32[]{:S(2)}) %copy-start.7) | copy-done | bytes 65560
  1.8 0.0 copy-done.8
  1.8 0.0 copy-done.9
  1.8 0.0 copy-done.10
  1.8 0.0 copy-start.1
  1.8 1.1 %copy-done.1 = f32[3,8,8192]{2,1,0:T(8,128)S(1)} copy-done((f32[3,8,8192]{2,1,0:T(8,128)S(1)}, f32[3,8,8192]{2,1,0:T(8,128)}, u32[]{:S(2)}) %copy-start.1) | copy-done | bytes 786456
  3.0 0.0 copy-start.2
  3.0 15.4 %prepare.1 = (f32[16,3,8,128]{3,2,1,0:T(8,128)S(1)}, f32[3,8,8192]{2,1,0:T(8,128)S(1)}, f32[3,8,512]{2,1,0:T(8,128)S(1)}, f32[3,8,512]{2,1,0:T(8,128)S(1)}, f32[...) custom-call(s32[128,128]{1,0:T(8,128)S(1)} %bitcast.7, f32[3,8,8192]{2,1,0:T(8,128)S(1)} %copy-done.1, ...), custom_call_target="tpu_custom_call" | custom-call | flops 805306368 | bytes 2359296 | tf_op jit(solution)/shard_map/prepare/pallas_call | solution.py:394
  18.4 0.0 copy-done.2
  18.4 0.0 copy-start.3
  18.4 0.0 copy-start.4
  18.4 0.0 copy-start.5
  18.4 0.1 broadcast_select_fusion.state_ref
  18.5 0.7 %copy-done.3 = s32[16384]{0:T(1024)S(1)} copy-done((s32[16384]{0:T(1024)S(1)}, s32[16384]{0:T(1024)}, u32[]{:S(2)}) %copy-start.3) | copy-done | bytes 65560
  19.2 0.0 copy-done.4
  19.2 0.0 copy-done.5
  19.3 28.1 %sweep.1 = (f32[3,8,4096]{2,1,0:T(8,128)S(1)}, f32[3,8192]{1,0:T(4,128)S(1)}) custom-call(f32[3,8,8192]{2,1,0:T(8,128)S(1)} %broadcast_select_fusion.state_ref, f32[3,8,512]{2,1,0:T(8,128)S(1)} %get-tuple-element.15.west_ref, f32[3,8,512]{2,1,0:T(8,128)S(1)} %get-tuple-element.16.east_ref, s32[24576]{0:T(1024)S(1)} %reshape.16.adjacent_ref, ...), custom_call_target="tpu_custom_call" | custom-call | tf_op jit(solution)/shard_map/sweep/pallas_call | solution.py:426
  47.4 1.3 %collective-permute-start = (f32[3,8,4096]{2,1,0:T(8,128)S(1)}, f32[3,8,4096]{2,1,0:T(8,128)S(1)}, u32[]{:S(2)}, u32[]{:S(2)}) collective-permute-start(f32[3,8,4096]{2,1,0:T(8,128)S(1)} %get-tuple-element.22.own_ref), channel_id=1, source_target_pairs={{0,16},{1,17},{2,18},{3,19},{4,20},{5,21},{6,22},{7,23},{8,24},{9,... | collective-permute-start | bytes 1179656 | tf_op jit(solution)/shard_map/ppermute | solution.py:444
  48.7 2.3 %collective-permute-done.helped_ref = f32[3,8,4096]{2,1,0:T(8,128)S(1)} collective-permute-done((f32[3,8,4096]{2,1,0:T(8,128)S(1)}, f32[3,8,4096]{2,1,0:T(8,128)S(1)}, u32[]{:S(2)}, u32[]{:S(2)}) %collective-permute-start) | collective-permute-done | bytes 393248 | tf_op jit(solution)/shard_map/ppermute | solution.py:444
  51.0 0.0 copy-start.6
  51.0 0.7 %copy-done.6 = f32[1,3]{1,0:T(1,128)S(1)} copy-done((f32[1,3]{1,0:T(1,128)S(1)}, f32[1,3]{1,0:T(1,128)}, u32[]{:S(2)}) %copy-start.6) | copy-done | bytes 36
  51.7 1.6 %finish.1 = f32[3,8,8192]{2,1,0:T(8,128)} custom-call(f32[3,8192]{1,0:T(4,128)S(1)} %get-tuple-element.18.regrid_ref, f32[1,3]{1,0:T(1,128)S(1)} %copy-done.6, f32[3,8,8192]{2,1,0:T(8,128)S(1)} %get-tuple-element.19.stepped_ref, f32[3,8,512]{2,1,0:T(8,128)S(1)} %get-tuple-element.20.west_ref, f32[3,8,512]{2,1,0:T(8,128)S(1)} %get-tuple-element.21.east_ref, ...), custom_call_target="tpu_custom_call" | custom-call | tf_op jit(solution)/shard_map/finish/pallas_call | solution.py:446
  (1 shorter events, 0.0 us)
Async XLA Ops:
  0.0 1.0 %copy-start = (s32[6,8192]{1,0:T(8,128)S(1)}, s32[6,8192]{1,0:T(8,128)}, u32[]{:S(2)}) copy-start(s32[6,8192]{1,0:T(8,128)} %param.17) | copy-start | bytes 589828
  1.0 0.8 %copy-start.7 = (s32[16384]{0:T(1024)S(1)}, s32[16384]{0:T(1024)}, u32[]{:S(2)}) copy-start(s32[16384]{0:T(1024)} %param.11) | copy-start | bytes 196612
  1.0 0.9 %copy-start.8 = (f32[2,8192]{1,0:T(2,128)S(1)}, f32[2,8192]{1,0:T(2,128)}, u32[]{:S(2)}) copy-start(f32[2,8192]{1,0:T(2,128)} %metric_ref.1) | copy-start | bytes 196612
  1.0 0.9 %copy-start.9 = (s32[2,512]{1,0:T(2,128)S(1)}, s32[2,512]{1,0:T(2,128)}, u32[]{:S(2)}) copy-start(s32[2,512]{1,0:T(2,128)} %edges_ref.1) | copy-start | bytes 12292
  1.1 0.8 %copy-start.10 = (f32[8]{0:T(128)S(1)}, f32[8]{0:T(128)}, u32[]{:S(2)}) copy-start(f32[8]{0:T(128)} %speed_ref.1) | copy-start | bytes 100
  1.8 1.1 %copy-start.1 = (f32[3,8,8192]{2,1,0:T(8,128)S(1)}, f32[3,8,8192]{2,1,0:T(8,128)}, u32[]{:S(2)}) copy-start(f32[3,8,8192]{2,1,0:T(8,128)} %state_ref.1) | copy-start | bytes 2359300
  3.0 15.4 %copy-start.2 = (f32[3,8,8192]{2,1,0:T(8,128)S(1)}, f32[3,8,8192]{2,1,0:T(8,128)}, u32[]{:S(2)}) copy-start(f32[3,8,8192]{2,1,0:T(8,128)} %state_ref.1) | copy-start | bytes 2359300
  18.4 0.8 %copy-start.3 = (s32[16384]{0:T(1024)S(1)}, s32[16384]{0:T(1024)}, u32[]{:S(2)}) copy-start(s32[16384]{0:T(1024)} %param.12) | copy-start | bytes 196612
  18.4 0.9 %copy-start.4 = (f32[16384]{0:T(1024)S(1)}, f32[16384]{0:T(1024)}, u32[]{:S(2)}) copy-start(f32[16384]{0:T(1024)} %param.13) | copy-start | bytes 196612
  18.4 0.9 %copy-start.5 = (f32[8192]{0:T(1024)S(1)}, f32[8192]{0:T(1024)}, u32[]{:S(2)}) copy-start(f32[8192]{0:T(1024)} %param.19) | copy-start | bytes 98308
  47.4 3.6 %collective-permute-start = (f32[3,8,4096]{2,1,0:T(8,128)S(1)}, f32[3,8,4096]{2,1,0:T(8,128)S(1)}, u32[]{:S(2)}, u32[]{:S(2)}) collective-permute-start(f32[3,8,4096]{2,1,0:T(8,128)S(1)} %get-tuple-element.22.own_ref), channel_id=1, source_target_pairs={{0,16},{1,17},{2,18},{3,19},{4,20},{5,21},{6,22},{7,23},{8,24},{9,... | collective-permute-start | bytes 1179656 | tf_op jit(solution)/shard_map/ppermute | solution.py:444
  51.0 0.7 %copy-start.6 = (f32[1,3]{1,0:T(1,128)S(1)}, f32[1,3]{1,0:T(1,128)}, u32[]{:S(2)}) copy-start(f32[1,3]{1,0:T(1,128)} %rate_ref.1) | copy-start | bytes 40
where the time goes:
time: 54 us; the launch traced here: 53.2 us
  Pallas kernels  45.1 us (84%)
  local copies, waits for them, and re-layouts  4.35 us (8%)
  waiting for transfers between devices  2.32 us (4%)
  starting transfers between devices  1.29 us (2%)
    pallas_call x1, Pallas kernels, body(): pl.pallas_call(sweep_kernel, out_shape=[jax.ShapeDtypeStruct((3, levels,...  28.1 us
    pallas_call x1, Pallas kernels, body(): pl.pallas_call(functools.partial(prepare_kernel, n, x_points, y_points),...  15.4 us
    unnamed x22, local copies, waits for them, and re-layouts  4.29 us
    ppermute x1, waiting for transfers between devices, body(): helped = lax.ppermute(swept, 'sec', [(0, 1)])  2.32 us
    pallas_call x1, Pallas kernels, body(): pl.pallas_call(functools.partial(finish_kernel, x_points, y_points), out_...  1.55 us
    ppermute x1, starting transfers between devices, body(): helped = lax.ppermute(swept, 'sec', [(0, 1)])  1.29 us
  transfers between devices with their start and end apart: 1, of which 1 were waited for; matrix products, arithmetic and copies ran while one was open for 0% of the time, Pallas kernels for 0%

commit v1 on v0

v1 whole, which is shorter than its diff:
```python
import functools
import jax
import jax.numpy as jnp
import numpy as np
from jax import lax
from jax.experimental import pallas as pl
from jax.experimental.pallas import tpu as pltpu
from jax.sharding import PartitionSpec as P

TIME_STEP = 0.05
LANES = 128
VMEM = pl.BlockSpec(memory_space=pltpu.VMEM)
SMEM = pl.BlockSpec(memory_space=pltpu.SMEM)
HBM = pl.BlockSpec(memory_space=pltpu.HBM)
PARAMS = dict(vmem_limit_bytes=24 << 20)


def gll_derivative():
    nodes = np.array([-1.0, -1.0 / np.sqrt(5.0), 1.0 / np.sqrt(5.0), 1.0])
    barycentric = np.array(
        [1.0 / np.prod([nodes[i] - nodes[j] for j in range(4) if j != i]) for i in range(4)]
    )
    matrix = np.zeros((4, 4))
    for i in range(4):
        for j in range(4):
            if i != j:
                matrix[i, j] = barycentric[j] / barycentric[i] / (nodes[i] - nodes[j])
        matrix[i, i] = -np.sum(matrix[i])
    return matrix


DERIVATIVE = gll_derivative()


def lane_phase(shape):
    return lax.broadcasted_iota(jnp.int32, shape, 1) % 4


def along_second(value, phase):
    width = value.shape[1]
    total = jnp.zeros_like(value)
    for shift in range(-3, 4):
        factor = jnp.zeros(value.shape, jnp.float32)
        for i in range(4):
            if 0 <= i + shift < 4:
                factor = jnp.where(phase == i, np.float32(DERIVATIVE[i, i + shift]), factor)
        moved = value if shift == 0 else pltpu.roll(value, (-shift) % width, 1)
        total = total + factor * moved
    return total


def advance(x_points, y_points, state_ref, metric_ref, speed_ref, stepped_ref):
    level = lax.broadcasted_iota(jnp.int32, (state_ref.shape[1], LANES), 0)
    speed = jnp.zeros(level.shape, jnp.float32)
    for k in range(level.shape[0]):
        speed = jnp.where(level == k, speed_ref[k], speed)

    def piece(g, _):
        def at(i, f):
            return state_ref[f, :, pl.ds(pl.multiple_of(start + i * y_points, LANES), LANES)]

        start = (g // (y_points // LANES)) * 4 * y_points + (g % (y_points // LANES)) * LANES
        phase = lane_phase((state_ref.shape[1], LANES))
        u = [at(i, 0) for i in range(4)]
        v = [at(i, 1) for i in range(4)]
        h = [at(i, 2) for i in range(4)]
        for i in range(4):
            here = pl.ds(pl.multiple_of(start + i * y_points, LANES), LANES)
            gx = metric_ref[0:1, here]
            gy = metric_ref[1:2, here]
            dx_h = sum(np.float32(DERIVATIVE[i, j]) * h[j] for j in range(4))
            dx_u = sum(np.float32(DERIVATIVE[i, j]) * u[j] for j in range(4))
            stepped_ref[0, :, here] = u[i] - TIME_STEP * (gx * dx_h)
            stepped_ref[1, :, here] = v[i] - TIME_STEP * (gy * along_second(h[i], phase))
            spread = gx * dx_u + gy * along_second(v[i], phase)
            stepped_ref[2, :, here] = h[i] - TIME_STEP * speed * spread
        return 0

    lax.fori_loop(0, x_points // 4 * (y_points // LANES), piece, 0)


CHUNK = 32
KEEP = 32


def two_terms(table):
    high = table.astype(jnp.bfloat16)
    low = (table - high.astype(jnp.float32)).astype(jnp.bfloat16)
    return jnp.concatenate([high, low], axis=1)


def pick(terms, depth, low, high):
    count = low.shape[1]
    low = jnp.broadcast_to(low.astype(jnp.int16), (LANES, count))
    lane = lax.broadcasted_iota(jnp.int16, (LANES, LANES), 0)
    lane = jnp.concatenate([lane] * (count // LANES), axis=1)
    hot = jnp.where(lane == low, jnp.bfloat16(1), jnp.bfloat16(0))
    found = jnp.dot(terms, jnp.concatenate([hot, hot], axis=0), preferred_element_type=jnp.float32)
    high = jnp.broadcast_to(high, (8, count))
    own = lax.broadcasted_iota(jnp.int32, high.shape, 0) == (high & 7)
    picked = []
    for f in range(3):
        parts = [found[f * depth + 8 * i : f * depth + 8 * i + 8] for i in range(depth // 8)]
        bit = 3
        while len(parts) > 1:
            odd = ((high >> bit) & 1) == 1
            parts = [jnp.where(odd, parts[i + 1], parts[i]) for i in range(0, len(parts), 2)]
            bit += 1
        picked.append(jnp.sum(jnp.where(own, parts[0], 0.0), axis=0, keepdims=True))
    return picked


def row_of(ref, start, count):
    return jnp.concatenate([ref[pl.ds(start + r, 1), :] for r in range(count)], axis=1)


def split_pairs(source_ref, weight_ref, low_ref, high_ref, share_ref):
    i = lax.broadcasted_iota(jnp.int32, (LANES, LANES), 0)
    j = lax.broadcasted_iota(jnp.int32, (LANES, LANES), 1)
    half = LANES // 2
    chosen = (i == 2 * (j % half) + j // half).astype(jnp.float32).astype(jnp.bfloat16)

    def move(value):
        return jnp.dot(value.astype(jnp.bfloat16), chosen, preferred_element_type=jnp.float32)

    source = source_ref[...]
    low_ref[...] = (move((source & (LANES - 1)).astype(jnp.float32)) + 0.5).astype(jnp.int32)
    high_ref[...] = (move((source >> 7).astype(jnp.float32)) + 0.5).astype(jnp.int32)
    weight = weight_ref[...]
    upper = weight.astype(jnp.bfloat16).astype(jnp.float32)
    share_ref[...] = move(upper) + move(weight - upper)


def regrid_into(regrid_ref, arrived, low_ref, high_ref, share_ref, terms_ref, value_ref):
    depth = low_ref.shape[0]
    for f in range(3):
        terms_ref[f * depth : (f + 1) * depth, :] = two_terms(arrived(f).reshape(depth, LANES))

    def step(c, _):
        low, high = row_of(low_ref, c * CHUNK, CHUNK), row_of(high_ref, c * CHUNK, CHUNK)
        values = pick(terms_ref[...], depth, low, high)
        for f in range(3):
            for r in range(CHUNK):
                value_ref[f, pl.ds(c * CHUNK + r, 1), :] = values[f][:, r * LANES : (r + 1) * LANES]
        return 0

    lax.fori_loop(0, depth // CHUNK, step, 0)
    share = share_ref[...]
    whole = share + pltpu.roll(share, LANES // 2, 1)
    first = lax.broadcasted_iota(jnp.int32, (depth // 2, LANES), 1) < LANES // 2
    for f in range(3):
        product = value_ref[f] * share
        share_ref[...] = (product + pltpu.roll(product, LANES // 2, 1)) / whole
        even = share_ref[pl.ds(0, depth // 2, stride=2), :]
        odd = share_ref[pl.ds(1, depth // 2, stride=2), :]
        regrid_ref[f] = jnp.where(first, even, odd)


def to_rows(source_ref, source_at, table_ref, table_at, count, name_at, unroll):
    def piece(c, _):
        here = pl.ds(pl.multiple_of(source_at + c * LANES, LANES), LANES)
        name = lax.broadcasted_iota(jnp.int32, (8, LANES), 1) + (name_at + c * LANES)
        kind = lax.broadcasted_iota(jnp.int32, (8, LANES), 0)
        name = jnp.where(kind < 6, name, jnp.where(kind == 6, 1, 0)).astype(jnp.float32)
        block = jnp.concatenate([source_ref[f, :, here] for f in range(3)] + [name], axis=0)
        there = pl.ds(pl.multiple_of(table_at + c * LANES, 8), LANES)
        table_ref[there, :KEEP] = jnp.transpose(block)
        return 0

    lax.fori_loop(0, count // LANES, piece, 0, unroll=unroll)


def walk(y_points, x_points, next_ref, edges_ref, visit, middle):
    def chain(c, _):
        base = pl.multiple_of(c * 16, 16)
        places = [edges_ref[0, base + u] for u in range(16)]
        for x in range(x_points - 1):
            if x or not middle:
                for u in range(16):
                    visit(x, base, u, places[u])
            if x < x_points - 2:
                places = [next_ref[place] for place in places]
        if not middle:
            for u in range(16):
                visit(x_points - 1, base, u, edges_ref[1, base + u])
        return 0

    lax.fori_loop(0, y_points // 16, chain, 0)


def start_kernel(
    n, x_points, y_points, state_hbm, rows_hbm, source_hbm, weight_hbm, metric_hbm, adjacent_hbm, edges_hbm, speed_hbm,
    state_ref, in_ref, regrid_ref, stepped_ref, west_ref, east_ref, table_ref, grid_ref,
    rows_ref, metric_ref, source_ref, weight_ref, low_ref, high_ref, share_ref, value_ref, made_ref,
    surface_ref, terms_ref, pair_terms_ref, out_ref, rim_ref, next_ref, edges_ref, speed_ref,
    load_sem, slot_send, slot_recv, edge_send, edge_recv, pair_send, pair_recv, made_send, made_recv,
):
    sec, dom = lax.axis_index("sec"), lax.axis_index("dom")
    right, left = lax.rem(dom + 1, n), lax.rem(dom + n - 1, n)
    mesh_ids = pl.DeviceIdType.MESH
    atmosphere, ocean = sec == 0, sec == 1
    load_state = pltpu.make_async_copy(state_hbm, state_ref, load_sem.at[0])
    load_rows = pltpu.make_async_copy(rows_hbm, rows_ref, load_sem.at[1])
    load_metric = pltpu.make_async_copy(metric_hbm, metric_ref, load_sem.at[2])
    load_next = pltpu.make_async_copy(adjacent_hbm.at[2], next_ref, load_sem.at[3])
    load_edges = pltpu.make_async_copy(edges_hbm, edges_ref, load_sem.at[4])
    load_speed = pltpu.make_async_copy(speed_hbm, speed_ref, load_sem.at[5])
    load_state.start()
    load_rows.start()
    barrier = pltpu.get_barrier_semaphore()

    def hello(a, b):
        pl.semaphore_signal(barrier, inc=1, device_id=(a, b), device_id_type=mesh_ids)

    @pl.when(atmosphere)
    def _():
        load_metric.start()
        load_speed.start()

        def greet(p, _):
            hello(1, p)

            @pl.when(p != dom)
            def _():
                hello(0, p)

            return 0

        lax.fori_loop(0, n, greet, 0)

    @pl.when(ocean)
    def _():
        load_edges.start()
        load_next.start()
        hello(0, dom)
        hello(1, left)
        hello(1, right)

    load_state.wait()
    depth, top = state_ref.shape[2] // LANES, state_ref.shape[1] - 1
    for f in range(3):
        for h in range(depth):
            surface_ref[f * depth + h : f * depth + h + 1, :] = state_ref[
                f, top : top + 1, h * LANES : (h + 1) * LANES
            ]
    terms_ref[...] = two_terms(surface_ref[...])
    load_rows.wait()

    def remote(source, target, send, recv, device):
        return pltpu.make_async_remote_copy(
            src_ref=source, dst_ref=target, send_sem=send, recv_sem=recv, device_id=device, device_id_type=mesh_ids
        )

    pair_source = remote(source_hbm, source_ref, pair_send.at[0], pair_recv.at[0], (0, dom))
    pair_weight = remote(weight_hbm, weight_ref, pair_send.at[1], pair_recv.at[1], (0, dom))

    @pl.when(atmosphere)
    def _():
        pl.semaphore_wait(barrier, n)

    @pl.when(ocean)
    def _():
        pl.semaphore_wait(barrier, n + 2)
        pair_source.start()
        pair_weight.start()

    lines = out_ref.shape[2]
    peers = CHUNK // lines

    def slots(p):
        return remote(out_ref.at[p], in_ref.at[sec, dom], slot_send.at[p], slot_recv.at[sec, dom], (0, p))

    def own_slots():
        return pltpu.make_async_copy(out_ref.at[dom], in_ref.at[0, dom], slot_recv.at[0, dom])

    chunks = rows_ref.shape[0] // CHUNK

    def send(k, _):
        c = lax.rem(k + dom * chunks // n, chunks)
        index = row_of(rows_ref, c * CHUNK, CHUNK)
        values = pick(terms_ref[...], depth, index & (LANES - 1), index >> 7)
        for f in range(3):
            for r in range(CHUNK):
                out_ref[c * peers + r // lines, f, pl.ds(r % lines, 1), :] = values[f][:, r * LANES : (r + 1) * LANES]

        def ship(j, _):
            p = c * peers + j
            here = jnp.logical_and(atmosphere, p == dom)

            @pl.when(here)
            def _():
                own_slots().start()

            @pl.when(jnp.logical_not(here))
            def _():
                slots(p).start()

            return 0

        lax.fori_loop(0, peers, ship, 0)
        return 0

    lax.fori_loop(0, chunks, send, 0)

    rows = state_ref.shape[2]
    first, last = pl.ds(0, y_points), pl.ds(rows - y_points, y_points)
    rim_first, rim_last = rim_ref.at[:, :, first], rim_ref.at[:, :, pl.ds(y_points, y_points)]
    air_edges = [
        remote(stepped_ref.at[:, :, last], west_ref, edge_send.at[0], edge_recv.at[0], (0, right)),
        remote(stepped_ref.at[:, :, first], east_ref, edge_send.at[1], edge_recv.at[1], (0, left)),
    ]
    sea_edges = [
        remote(rim_last, west_ref, edge_send.at[0], edge_recv.at[0], (1, right)),
        remote(rim_first, east_ref, edge_send.at[1], edge_recv.at[1], (1, left)),
    ]
    made = remote(made_ref, regrid_ref, made_send, made_recv, (1, dom))

    def sent(p, _):
        @pl.when(jnp.logical_not(jnp.logical_and(atmosphere, p == dom)))
        def _():
            slots(p).wait_send()

        return 0

    def arrived_from(a):
        def wait(p, _):
            def arrival():
                remote(out_ref.at[p], in_ref.at[a, p], slot_send.at[p], slot_recv.at[a, p], (0, p)).wait_recv()

            if a:
                arrival()
            else:

                @pl.when(p == dom)
                def _():
                    own_slots().wait()

                @pl.when(p != dom)
                def _():
                    arrival()

            return 0

        lax.fori_loop(0, n, wait, 0)

    @pl.when(atmosphere)
    def _():
        load_metric.wait()
        load_speed.wait()
        advance(x_points, y_points, state_ref, metric_ref, speed_ref, stepped_ref)
        for each in air_edges:
            each.start()
        pair_source.wait_recv()
        pair_weight.wait_recv()
        split_pairs(source_ref, weight_ref, low_ref, high_ref, share_ref)
        arrived_from(0)
        regrid_into(made_ref, lambda f: in_ref[0, :, f], low_ref, high_ref, share_ref, pair_terms_ref, value_ref)
        made.start()
        arrived_from(1)
        for each in air_edges:
            each.wait()
        lax.fori_loop(0, n, sent, 0)
        made.wait_send()

    @pl.when(ocean)
    def _():
        to_rows(state_ref, 0, table_ref, 0, rows, 0, 8)
        load_edges.wait()

        def column(x, u):
            return pl.ds(8 + (x + 1) * y_points + u, 1)

        def edge(c, _):
            base = pl.multiple_of(c * 16, 16)
            for k, x in ((0, 0), (1, x_points - 1)):
                places = [edges_ref[k, base + u] for u in range(16)]
                for u in range(16):
                    grid_ref[column(x, base + u), :] = table_ref[pl.ds(places[u], 1), :]
            return 0

        lax.fori_loop(0, y_points // 16, edge, 0)
        for k, x in ((0, 0), (1, x_points - 1)):
            for c in range(y_points // LANES):
                at = 8 + (x + 1) * y_points + c * LANES
                block = jnp.transpose(grid_ref[at : at + LANES, :KEEP])
                for f in range(3):
                    levels = top + 1
                    rim_ref[f, :, k * y_points + c * LANES : k * y_points + (c + 1) * LANES] = block[
                        f * levels : (f + 1) * levels
                    ]
        for each in sea_edges:
            each.start()
        load_next.wait()

        def visit(x, base, u, place):
            grid_ref[column(x, base + u), :] = table_ref[pl.ds(place, 1), :]

        walk(y_points, x_points, next_ref, edges_ref, visit, True)
        pair_source.wait_send()
        pair_weight.wait_send()
        for each in sea_edges:
            each.wait()
        lax.fori_loop(0, n, sent, 0)
        made.wait_recv()


def sum_neighbours(x_points, y_points, grid_ref, rims, sum_ref):
    lane = lax.broadcasted_iota(jnp.int32, (8, LANES), 1)
    row = lax.broadcasted_iota(jnp.int32, (8, LANES), 0)

    def mask(*names):
        kept = lane < 24
        for name in names:
            kept = kept | (lane == 24 + name)
        return kept.astype(jnp.float32)

    same, tilted = mask(2, 3), mask(4, 5)
    above, below = mask(0), mask(1)
    east, west = mask(2, 4), mask(3, 5)

    def read(x, at, shift):
        if 0 <= x < x_points:
            return grid_ref[pl.ds(8 + (x + 1) * y_points + at + shift, 8), :]
        return rims[0 if x < 0 else 1][pl.ds(8 + at + shift, 8), :]

    def inner(c, _):
        at = c * 8
        joined = {}
        for x in range(-1, x_points + 1):
            tilt = -1 if x % 2 else 1
            joined[x] = read(x, at, 0) * same + read(x, at, tilt) * tilted
            if x > 0:
                upright = read(x - 1, at, 1) * above + read(x - 1, at, -1) * below
                total = upright + joined[x] * east + joined[x - 2] * west
                sum_ref[pl.ds(pl.multiple_of((x - 1) * y_points + at, 8), 8), :] = total
        return 0

    lax.fori_loop(1, y_points // 8 - 1, inner, 0)

    for at, gone, missing in ((0, row == 0, -1), (y_points - 8, row == 7, 1)):
        for x in range(x_points):
            own = read(x, at, 0)
            tilt = 1 if x % 2 else -1

            def near(x, shift):
                value = read(x, at, shift)
                return jnp.where(gone, own, value) if shift == missing else value

            total = near(x, 1) * above + near(x, -1) * below
            total = total + (near(x + 1, 0) * same + near(x + 1, tilt) * tilted) * east
            total = total + (near(x - 1, 0) * same + near(x - 1, tilt) * tilted) * west
            sum_ref[x * y_points + at : x * y_points + at + 8, :] = total


def end_kernel(
    x_points, y_points, state_ref, in_ref, regrid_in_ref, stepped_ref, west_ref, east_ref, table_in_ref, grid_ref,
    source_hbm, weight_hbm, kappa_hbm, adjacent_hbm, edges_hbm, rate_hbm,
    new_hbm, table_ref,
    new_ref, source_ref, weight_ref, low_ref, high_ref, share_ref, value_ref, pair_terms_ref, regrid_ref,
    kappa_ref, adjacent_ref, next_ref, few_ref, west_rim_ref, east_rim_ref, sum_ref, edges_ref, rate_ref,
    load_sem, store_sem,
):
    sec = lax.axis_index("sec")
    load_rate = pltpu.make_async_copy(rate_hbm, rate_ref, load_sem.at[5])
    load_rate.start()
    levels, rows = state_ref.shape[1], state_ref.shape[2]

    def couple(f, here, value, relaxed):
        row = lax.broadcasted_iota(jnp.int32, value.shape, 0)
        new_ref[f, :, here] = jnp.where(row == levels - 1, value + rate_ref[0, f] * (relaxed - value), value)

    @pl.when(sec == 0)
    def _():
        load_source = pltpu.make_async_copy(source_hbm, source_ref, load_sem.at[0])
        load_weight = pltpu.make_async_copy(weight_hbm, weight_ref, load_sem.at[1])
        load_source.start()
        load_weight.start()
        load_source.wait()
        load_weight.wait()
        load_rate.wait()
        split_pairs(source_ref, weight_ref, low_ref, high_ref, share_ref)
        regrid_into(regrid_ref, lambda f: in_ref[1, :, f], low_ref, high_ref, share_ref, pair_terms_ref, value_ref)
        stores = [pltpu.make_async_copy(new_ref.at[f], new_hbm.at[f], store_sem.at[f]) for f in range(3)]
        for f in range(3):
            for x in range(x_points):
                here = slice(x * y_points, (x + 1) * y_points)
                value = stepped_ref[f, :, here]
                if x % 4 == 3:
                    other = (
                        stepped_ref[f, :, (x + 1) * y_points : (x + 2) * y_points]
                        if x < x_points - 1
                        else east_ref[f]
                    )
                    value = (value + other) * 0.5
                elif x % 4 == 0:
                    other = stepped_ref[f, :, (x - 1) * y_points : x * y_points] if x else west_ref[f]
                    value = (value + other) * 0.5
                position = lax.broadcasted_iota(jnp.int32, value.shape, 1)
                phase = position % 4
                after = pltpu.roll(value, y_points - 1, 1)
                before = pltpu.roll(value, 1, 1)
                averaged = jnp.where(
                    (phase == 3) & (position < y_points - 1),
                    (value + after) * 0.5,
                    jnp.where((phase == 0) & (position > 0), (value + before) * 0.5, value),
                )
                lines = y_points // LANES
                relaxed = jnp.concatenate(
                    [regrid_ref[f, x * lines + i : x * lines + i + 1, :] for i in range(lines)], axis=1
                )
                couple(f, here, averaged, relaxed)
            stores[f].start()
        for each in stores:
            each.wait()

    @pl.when(sec == 1)
    def _():
        load_next = pltpu.make_async_copy(adjacent_hbm.at[2], next_ref, load_sem.at[0])
        load_adjacent = pltpu.make_async_copy(adjacent_hbm, adjacent_ref, load_sem.at[1])
        load_kappa = pltpu.make_async_copy(kappa_hbm, kappa_ref, load_sem.at[2])
        load_edges = pltpu.make_async_copy(edges_hbm, edges_ref, load_sem.at[4])
        load_edges.start()
        load_next.start()
        load_adjacent.start()
        load_kappa.start()
        to_rows(west_ref, 0, west_rim_ref, 8, y_points, rows, 4)
        to_rows(east_ref, 0, east_rim_ref, 8, y_points, rows + y_points, 4)
        sum_neighbours(x_points, y_points, grid_ref, (west_rim_ref, east_rim_ref), sum_ref)
        load_next.wait()
        load_edges.wait()
        load_rate.wait()

        def visit(x, base, u, place):
            table_ref[pl.ds(place, 1), :] = sum_ref[pl.ds(x * y_points + base + u, 1), :]

        walk(y_points, x_points, next_ref, edges_ref, visit, False)
        load_adjacent.wait()
        load_kappa.wait()
        part = rows // 4
        stores = [
            pltpu.make_async_copy(
                new_ref.at[:, :, pl.ds(k * part, part)], new_hbm.at[:, :, pl.ds(k * part, part)], store_sem.at[k]
            )
            for k in range(4)
        ]

        def finish(c, wrong):
            here = pl.ds(pl.multiple_of(c * LANES, LANES), LANES)
            block = jnp.transpose(table_ref[here, :KEEP])
            kappa = kappa_ref[pl.ds(c, 1), :]
            for f in range(3):
                value = state_ref[f, :, here]
                swept = value + kappa * (block[f * levels : (f + 1) * levels] - 6.0 * value)
                couple(f, here, swept, regrid_in_ref[f, pl.ds(c, 1), :])
            named = adjacent_ref[:, here].astype(jnp.float32)
            names = block[24:32]
            off = (names[0:6] != named).astype(jnp.float32)
            return jnp.maximum(wrong, jnp.maximum(jnp.max(off, axis=0, keepdims=True), names[6:7]))

        wrong = jnp.zeros((1, LANES), jnp.float32)
        for k in range(4):
            blocks = part // LANES
            wrong = lax.fori_loop(k * blocks, (k + 1) * blocks, finish, wrong, unroll=8)
            stores[k].start()
        for each in stores:
            each.wait()

        @pl.when(jnp.max(wrong) > 0.0)
        def _():
            to_rows(state_ref, 0, sum_ref, 0, rows, 0, 1)
            to_rows(west_ref, 0, sum_ref, rows, y_points, rows, 1)
            to_rows(east_ref, 0, sum_ref, rows + y_points, y_points, rows + y_points, 1)

            def block(c, _):
                fetch = pltpu.make_async_copy(
                    adjacent_hbm.at[:, pl.ds(pl.multiple_of(c * LANES, LANES), LANES)], few_ref, load_sem.at[3]
                )
                fetch.start()
                fetch.wait()

                def cell(i, _):
                    total = sum_ref[pl.ds(few_ref[0, i], 1), :]
                    for j in range(1, 6):
                        total = total + sum_ref[pl.ds(few_ref[j, i], 1), :]
                    table_ref[pl.ds(c * LANES + i, 1), :] = total
                    return 0

                lax.fori_loop(0, LANES, cell, 0)
                return 0

            lax.fori_loop(0, rows // LANES, block, 0)
            lax.fori_loop(0, rows // LANES, finish, wrong)
            whole = pltpu.make_async_copy(new_ref, new_hbm, store_sem.at[0])
            whole.start()
            whole.wait()


def body(
    state, send_rows, intersection_source, intersection_weight, couple_rate, atm_metric, wave_speed,
    ocean_adjacent, ocean_edges, ocean_kappa,
):
    levels, rows = state.shape[1], state.shape[2]
    y_points = ocean_edges.shape[1]
    x_points = rows // y_points
    n = lax.axis_size("dom")
    slots = send_rows.shape[0]
    lines = slots // n // LANES
    f32, i32 = jnp.float32, jnp.int32
    pairs = slots // LANES
    source, weight = intersection_source.reshape(-1, LANES), intersection_weight.reshape(-1, LANES)
    placed, slot_rows, source, weight, metric, adjacent, kappa, edges, speed, rate = [
        pltpu.with_memory_space_constraint(each, pltpu.HBM)
        for each in (
            state, send_rows.reshape(-1, LANES), source, weight, atm_metric, ocean_adjacent,
            ocean_kappa.reshape(-1, LANES), ocean_edges, wave_speed, couple_rate,
        )
    ]

    border = jax.ShapeDtypeStruct((3, levels, y_points), f32)
    whole = jax.ShapeDtypeStruct(state.shape, f32)
    table = jax.ShapeDtypeStruct((rows, LANES), f32)
    made = jax.ShapeDtypeStruct((3, rows // LANES, LANES), f32)
    pair_scratch = [
        pltpu.VMEM((pairs, LANES), i32),
        pltpu.VMEM((pairs, LANES), f32),
        pltpu.VMEM((pairs, LANES), i32),
        pltpu.VMEM((pairs, LANES), i32),
        pltpu.VMEM((pairs, LANES), f32),
        pltpu.VMEM((3, pairs, LANES), f32),
    ]
    dma = pltpu.SemaphoreType.DMA
    held, incoming, regrid, stepped, west, east, cells, grid = pl.pallas_call(
        functools.partial(start_kernel, n, x_points, y_points),
        out_shape=[
            whole,
            jax.ShapeDtypeStruct((2, n, 3, lines, LANES), f32),
            made,
            whole,
            border,
            border,
            table,
            jax.ShapeDtypeStruct(((x_points + 2) * y_points + 16, LANES), f32),
        ],
        in_specs=[HBM] * 8,
        out_specs=[VMEM] * 8,
        scratch_shapes=[
            pltpu.VMEM((pairs, LANES), i32),
            pltpu.VMEM(atm_metric.shape, f32),
            *pair_scratch,
            pltpu.VMEM(made.shape, f32),
            pltpu.VMEM((3 * rows // LANES, LANES), f32),
            pltpu.VMEM((3 * rows // LANES, 2 * LANES), jnp.bfloat16),
            pltpu.VMEM((3 * pairs, 2 * LANES), jnp.bfloat16),
            pltpu.VMEM((n, 3, lines, LANES), f32),
            pltpu.VMEM((3, levels, 2 * y_points), f32),
            pltpu.SMEM((rows,), i32),
            pltpu.SMEM(ocean_edges.shape, i32),
            pltpu.SMEM(wave_speed.shape, f32),
            dma((6,)),
            dma((n,)),
            dma((2, n)),
            dma((2,)),
            dma((2,)),
            dma((2,)),
            dma((2,)),
            dma,
            dma,
        ],
        compiler_params=pltpu.CompilerParams(collective_id=0, has_side_effects=True, **PARAMS),
        name="start",
    )(
        placed, slot_rows, source, weight, metric, adjacent, edges, speed,
    )

    new_state, _ = pl.pallas_call(
        functools.partial(end_kernel, x_points, y_points),
        out_shape=[whole, table],
        in_specs=[VMEM] * 8 + [HBM] * 6,
        out_specs=[HBM, VMEM],
        input_output_aliases={6: 1},
        scratch_shapes=[
            pltpu.VMEM(state.shape, f32),
            *pair_scratch,
            pltpu.VMEM((3 * pairs, 2 * LANES), jnp.bfloat16),
            pltpu.VMEM(made.shape, f32),
            pltpu.VMEM((rows // LANES, LANES), f32),
            pltpu.VMEM(ocean_adjacent.shape, i32),
            pltpu.SMEM((rows,), i32),
            pltpu.SMEM((6, LANES), i32),
            pltpu.VMEM((y_points + 16, LANES), f32),
            pltpu.VMEM((y_points + 16, LANES), f32),
            pltpu.VMEM((rows + 2 * y_points, LANES), f32),
            pltpu.SMEM(ocean_edges.shape, i32),
            pltpu.SMEM(couple_rate.shape, f32),
            dma((6,)),
            dma((4,)),
        ],
        compiler_params=pltpu.CompilerParams(**PARAMS),
        name="end",
    )(
        held, incoming, regrid, stepped, west, east, cells, grid,
        source, weight, kappa, adjacent, edges, rate,
    )
    return new_state


def solution(mesh):
    in_specs = (
        P(None, None, ("sec", "dom")),
        P(("sec", "dom")),
        P(("sec", "dom")),
        P(("sec", "dom")),
        P("sec", None),
        P(None, "dom"),
        P(),
        P(None, "dom"),
        P(None, "dom"),
        P("dom"),
    )
    out_specs = P(None, None, ("sec", "dom"))
    return jax.shard_map(body, mesh=mesh, in_specs=in_specs, out_specs=out_specs, check_vma=False)
```

time: 54 us -> 30 us (0.56); the launches traced: 53.2 us -> 29.9 us
  Pallas kernels: 45.1 us -> 29.8 us
  local copies, waits for them, and re-layouts: 4.35 us -> 0 us
  waiting for transfers between devices: 2.32 us -> 0 us
  starting transfers between devices: 1.29 us -> 0 us
    pallas_call x3 -> x2, Pallas kernels: 45.1 us -> 29.8 us  [the longest x1 19.2 us: body(): pl.pallas_call(functools.partial(start_kernel, n, x_points, y_points), ou...]
    unnamed x22 -> x0, local copies, waits for them, and re-layouts: 4.29 us -> none
    ppermute x1 -> x0, waiting for transfers between devices: 2.32 us -> none  [body(): helped = lax.ppermute(swept, 'sec', [(0, 1)])]
    ppermute x1 -> x0, starting transfers between devices: 1.29 us -> none  [body(): helped = lax.ppermute(swept, 'sec', [(0, 1)])]
  transfers between devices with their start and end apart: 1 -> 0, of which waited for: 1 -> 0; matrix products, arithmetic and copies ran while one was open for 0% -> 0% of each run, Pallas kernels for 0% -> 0%
where the time goes in v1:
time: 30 us; the launch traced here: 29.9 us
  Pallas kernels  29.8 us (99%)
    pallas_call x1, Pallas kernels, body(): pl.pallas_call(functools.partial(start_kernel, n, x_points, y_points), ou...  19.2 us
    pallas_call x1, Pallas kernels, body(): pl.pallas_call(functools.partial(end_kernel, x_points, y_points), out_sha...  10.6 us

profile of v1, /device:TPU:1, one launch (start us, length us, event | category | flops | bytes accessed | tf_op | source)
XLA Modules:
  0.0 29.9 jit_solution(6451639542786607797)
XLA Ops:
  0.0 19.2 %start.1 = (f32[3,8,8192]{2,1,0:T(8,128)S(1)}, f32[2,16,3,8,128]{4,3,2,1,0:T(8,128)S(1)}, f32[3,64,128]{2,1,0:T(8,128)S(1)}, f32[3,8,8192]{2,1,0:T(8,128)S(1)}, ...) custom-call(f32[3,8,8192]{2,1,0:T(8,128)} %state_hbm.1, ...), custom_call_target="tpu_custom_call" | custom-call | tf_op jit(solution)/shard_map/start/pallas_call | solution.py:632
  19.2 10.6 %end.1 = (f32[3,8,8192]{2,1,0:T(8,128)}, f32[8192,128]{1,0:T(8,128)S(1)}) custom-call(f32[3,8,8192]{2,1,0:T(8,128)S(1)} %get-tuple-element.14.state_ref, f32[2,16,3,8,128]{4,3,2,1,0:T(8,128)S(1)} %get-tuple-element.15.in_ref, f32[3,64,128]{2,1,0:T(8,128)S(1)} %get-tuple-element.16.regrid_in_ref, ...), custom_call_target="tpu_custom_call", output_to_operand_aliasing={{1}: (6, {})} | custom-call | tf_op jit(solution)/shard_map/end/pallas_call | solution.py:675

commit v2 on v1

--- a/solution.py
+++ b/solution.py
@@ -131,7 +131,7 @@
     share_ref[...] = move(upper) + move(weight - upper)
 
 
-def regrid_into(regrid_ref, arrived, low_ref, high_ref, share_ref, terms_ref, value_ref):
+def regrid_into(regrid_ref, arrived, low_ref, high_ref, share_ref, terms_ref, value_ref, ratio_ref):
     depth = low_ref.shape[0]
     for f in range(3):
         terms_ref[f * depth : (f + 1) * depth, :] = two_terms(arrived(f).reshape(depth, LANES))
@@ -150,9 +150,9 @@
     first = lax.broadcasted_iota(jnp.int32, (depth // 2, LANES), 1) < LANES // 2
     for f in range(3):
         product = value_ref[f] * share
-        share_ref[...] = (product + pltpu.roll(product, LANES // 2, 1)) / whole
-        even = share_ref[pl.ds(0, depth // 2, stride=2), :]
-        odd = share_ref[pl.ds(1, depth // 2, stride=2), :]
+        ratio_ref[...] = (product + pltpu.roll(product, LANES // 2, 1)) / whole
+        even = ratio_ref[pl.ds(0, depth // 2, stride=2), :]
+        odd = ratio_ref[pl.ds(1, depth // 2, stride=2), :]
         regrid_ref[f] = jnp.where(first, even, odd)
 
 
@@ -170,19 +170,17 @@
     lax.fori_loop(0, count // LANES, piece, 0, unroll=unroll)
 
 
-def walk(y_points, x_points, next_ref, edges_ref, visit, middle):
+def walk(y_points, x_points, next_ref, first_ref, last_ref, visit, middle):
     def chain(c, _):
         base = pl.multiple_of(c * 16, 16)
-        places = [edges_ref[0, base + u] for u in range(16)]
+        places = [first_ref[base + u] for u in range(16)]
         for x in range(x_points - 1):
             if x or not middle:
-                for u in range(16):
-                    visit(x, base, u, places[u])
+                visit(x, base, places)
             if x < x_points - 2:
                 places = [next_ref[place] for place in places]
         if not middle:
-            for u in range(16):
-                visit(x_points - 1, base, u, edges_ref[1, base + u])
+            visit(x_points - 1, base, [last_ref[base + u] for u in range(16)])
         return 0
 
     lax.fori_loop(0, y_points // 16, chain, 0)
@@ -190,9 +188,10 @@
 
 def start_kernel(
     n, x_points, y_points, state_hbm, rows_hbm, source_hbm, weight_hbm, metric_hbm, adjacent_hbm, edges_hbm, speed_hbm,
-    state_ref, in_ref, regrid_ref, stepped_ref, west_ref, east_ref, table_ref, grid_ref,
-    rows_ref, metric_ref, source_ref, weight_ref, low_ref, high_ref, share_ref, value_ref, made_ref,
-    surface_ref, terms_ref, pair_terms_ref, out_ref, rim_ref, next_ref, edges_ref, speed_ref,
+    state_ref, in_ref, regrid_ref, stepped_ref, west_ref, east_ref, table_ref, sum_ref, low_ref, high_ref, share_ref,
+    rows_ref, metric_ref, source_ref, weight_ref, sea_source_ref, sea_weight_ref, sea_low_ref, sea_high_ref,
+    sea_share_ref, value_ref, ratio_ref, pair_terms_ref, made_ref, surface_ref, terms_ref, out_ref, rim_ref, grid_ref,
+    west_rim_ref, east_rim_ref, next_ref, first_ref, last_ref, speed_ref,
     load_sem, slot_send, slot_recv, edge_send, edge_recv, pair_send, pair_recv, made_send, made_recv,
 ):
     sec, dom = lax.axis_index("sec"), lax.axis_index("dom")
@@ -203,8 +202,11 @@
     load_rows = pltpu.make_async_copy(rows_hbm, rows_ref, load_sem.at[1])
     load_metric = pltpu.make_async_copy(metric_hbm, metric_ref, load_sem.at[2])
     load_next = pltpu.make_async_copy(adjacent_hbm.at[2], next_ref, load_sem.at[3])
-    load_edges = pltpu.make_async_copy(edges_hbm, edges_ref, load_sem.at[4])
+    load_first = pltpu.make_async_copy(edges_hbm.at[0], first_ref, load_sem.at[4])
+    load_last = pltpu.make_async_copy(edges_hbm.at[1], last_ref, load_sem.at[8])
     load_speed = pltpu.make_async_copy(speed_hbm, speed_ref, load_sem.at[5])
+    load_source = pltpu.make_async_copy(source_hbm, source_ref, load_sem.at[6])
+    load_weight = pltpu.make_async_copy(weight_hbm, weight_ref, load_sem.at[7])
     load_state.start()
     load_rows.start()
     barrier = pltpu.get_barrier_semaphore()
@@ -214,9 +216,6 @@
 
     @pl.when(atmosphere)
     def _():
-        load_metric.start()
-        load_speed.start()
-
         def greet(p, _):
             hello(1, p)
 
@@ -227,17 +226,54 @@
             return 0
 
         lax.fori_loop(0, n, greet, 0)
+        load_metric.start()
+        load_speed.start()
+        load_source.start()
+        load_weight.start()
 
     @pl.when(ocean)
     def _():
-        load_edges.start()
-        load_next.start()
         hello(0, dom)
         hello(1, left)
         hello(1, right)
+        load_first.start()
+        load_last.start()
+        load_next.start()
 
     load_state.wait()
-    depth, top = state_ref.shape[2] // LANES, state_ref.shape[1] - 1
+    depth, top, rows = state_ref.shape[2] // LANES, state_ref.shape[1] - 1, state_ref.shape[2]
+
+    def column(x, u):
+        return pl.ds(8 + (x + 1) * y_points + u, 1)
+
+    def visit(x, base, places):
+        found = [table_ref[pl.ds(place, 1), :] for place in places]
+        for u in range(len(places)):
+            grid_ref[column(x, base + u), :] = found[u]
+
+    @pl.when(ocean)
+    def _():
+        to_rows(state_ref, 0, table_ref, 0, rows, 0, 8)
+        load_first.wait()
+        load_last.wait()
+
+        def edge(c, _):
+            base = pl.multiple_of(c * 16, 16)
+            for listed, x in ((first_ref, 0), (last_ref, x_points - 1)):
+                visit(x, base, [listed[base + u] for u in range(16)])
+            return 0
+
+        lax.fori_loop(0, y_points // 16, edge, 0)
+        levels = top + 1
+        for k, x in ((0, 0), (1, x_points - 1)):
+            for c in range(y_points // LANES):
+                at = 8 + (x + 1) * y_points + c * LANES
+                block = jnp.transpose(grid_ref[at : at + LANES, :KEEP])
+                for f in range(3):
+                    rim_ref[f, :, k * y_points + c * LANES : k * y_points + (c + 1) * LANES] = block[
+                        f * levels : (f + 1) * levels
+                    ]
+
     for f in range(3):
         for h in range(depth):
             surface_ref[f * depth + h : f * depth + h + 1, :] = state_ref[
@@ -251,21 +287,9 @@
             src_ref=source, dst_ref=target, send_sem=send, recv_sem=recv, device_id=device, device_id_type=mesh_ids
         )
 
-    pair_source = remote(source_hbm, source_ref, pair_send.at[0], pair_recv.at[0], (0, dom))
-    pair_weight = remote(weight_hbm, weight_ref, pair_send.at[1], pair_recv.at[1], (0, dom))
-
-    @pl.when(atmosphere)
-    def _():
-        pl.semaphore_wait(barrier, n)
-
-    @pl.when(ocean)
-    def _():
-        pl.semaphore_wait(barrier, n + 2)
-        pair_source.start()
-        pair_weight.start()
-
     lines = out_ref.shape[2]
     peers = CHUNK // lines
+    chunks = rows_ref.shape[0] // CHUNK
 
     def slots(p):
         return remote(out_ref.at[p], in_ref.at[sec, dom], slot_send.at[p], slot_recv.at[sec, dom], (0, p))
@@ -273,7 +297,9 @@
     def own_slots():
         return pltpu.make_async_copy(out_ref.at[dom], in_ref.at[0, dom], slot_recv.at[0, dom])
 
-    chunks = rows_ref.shape[0] // CHUNK
+    pair_source = remote(source_hbm, sea_source_ref, pair_send.at[0], pair_recv.at[0], (0, dom))
+    pair_weight = remote(weight_hbm, sea_weight_ref, pair_send.at[1], pair_recv.at[1], (0, dom))
+    made = remote(made_ref, regrid_ref, made_send, made_recv, (1, dom))
 
     def send(k, _):
         c = lax.rem(k + dom * chunks // n, chunks)
@@ -283,6 +309,16 @@
             for r in range(CHUNK):
                 out_ref[c * peers + r // lines, f, pl.ds(r % lines, 1), :] = values[f][:, r * LANES : (r + 1) * LANES]
 
+        @pl.when(jnp.logical_and(k == 0, atmosphere))
+        def _():
+            pl.semaphore_wait(barrier, n)
+
+        @pl.when(jnp.logical_and(k == 0, ocean))
+        def _():
+            pl.semaphore_wait(barrier, n + 2)
+            pair_source.start()
+            pair_weight.start()
+
         def ship(j, _):
             p = c * peers + j
             here = jnp.logical_and(atmosphere, p == dom)
@@ -302,7 +338,6 @@
 
     lax.fori_loop(0, chunks, send, 0)
 
-    rows = state_ref.shape[2]
     first, last = pl.ds(0, y_points), pl.ds(rows - y_points, y_points)
     rim_first, rim_last = rim_ref.at[:, :, first], rim_ref.at[:, :, pl.ds(y_points, y_points)]
     air_edges = [
@@ -313,7 +348,6 @@
         remote(rim_last, west_ref, edge_send.at[0], edge_recv.at[0], (1, right)),
         remote(rim_first, east_ref, edge_send.at[1], edge_recv.at[1], (1, left)),
     ]
-    made = remote(made_ref, regrid_ref, made_send, made_recv, (1, dom))
 
     def sent(p, _):
         @pl.when(jnp.logical_not(jnp.logical_and(atmosphere, p == dom)))
@@ -322,26 +356,8 @@
 
         return 0
 
-    def arrived_from(a):
-        def wait(p, _):
-            def arrival():
-                remote(out_ref.at[p], in_ref.at[a, p], slot_send.at[p], slot_recv.at[a, p], (0, p)).wait_recv()
-
-            if a:
-                arrival()
-            else:
-
-                @pl.when(p == dom)
-                def _():
-                    own_slots().wait()
-
-                @pl.when(p != dom)
-                def _():
-                    arrival()
-
-            return 0
-
-        lax.fori_loop(0, n, wait, 0)
+    def arrival(a, p):
+        remote(out_ref.at[p], in_ref.at[a, p], slot_send.at[p], slot_recv.at[a, p], (0, p)).wait_recv()
 
     @pl.when(atmosphere)
     def _():
@@ -350,13 +366,36 @@
         advance(x_points, y_points, state_ref, metric_ref, speed_ref, stepped_ref)
         for each in air_edges:
             each.start()
+        load_source.wait()
+        load_weight.wait()
+        split_pairs(source_ref, weight_ref, low_ref, high_ref, share_ref)
         pair_source.wait_recv()
         pair_weight.wait_recv()
-        split_pairs(source_ref, weight_ref, low_ref, high_ref, share_ref)
-        arrived_from(0)
-        regrid_into(made_ref, lambda f: in_ref[0, :, f], low_ref, high_ref, share_ref, pair_terms_ref, value_ref)
+        split_pairs(sea_source_ref, sea_weight_ref, sea_low_ref, sea_high_ref, sea_share_ref)
+
+        def from_air(p, _):
+            @pl.when(p == dom)
+            def _():
+                own_slots().wait()
+
+            @pl.when(p != dom)
+            def _():
+                arrival(0, p)
+
+            return 0
+
+        lax.fori_loop(0, n, from_air, 0)
+        regrid_into(
+            made_ref, lambda f: in_ref[0, :, f], sea_low_ref, sea_high_ref, sea_share_ref,
+            pair_terms_ref, value_ref, ratio_ref,
+        )
         made.start()
-        arrived_from(1)
+
+        def from_sea(p, _):
+            arrival(1, p)
+            return 0
+
+        lax.fori_loop(0, n, from_sea, 0)
         for each in air_edges:
             each.wait()
         lax.fori_loop(0, n, sent, 0)
@@ -364,42 +403,17 @@
 
     @pl.when(ocean)
     def _():
-        to_rows(state_ref, 0, table_ref, 0, rows, 0, 8)
-        load_edges.wait()
-
-        def column(x, u):
-            return pl.ds(8 + (x + 1) * y_points + u, 1)
-
-        def edge(c, _):
-            base = pl.multiple_of(c * 16, 16)
-            for k, x in ((0, 0), (1, x_points - 1)):
-                places = [edges_ref[k, base + u] for u in range(16)]
-                for u in range(16):
-                    grid_ref[column(x, base + u), :] = table_ref[pl.ds(places[u], 1), :]
-            return 0
-
-        lax.fori_loop(0, y_points // 16, edge, 0)
-        for k, x in ((0, 0), (1, x_points - 1)):
-            for c in range(y_points // LANES):
-                at = 8 + (x + 1) * y_points + c * LANES
-                block = jnp.transpose(grid_ref[at : at + LANES, :KEEP])
-                for f in range(3):
-                    levels = top + 1
-                    rim_ref[f, :, k * y_points + c * LANES : k * y_points + (c + 1) * LANES] = block[
-                        f * levels : (f + 1) * levels
-                    ]
         for each in sea_edges:
             each.start()
         load_next.wait()
-
-        def visit(x, base, u, place):
-            grid_ref[column(x, base + u), :] = table_ref[pl.ds(place, 1), :]
-
-        walk(y_points, x_points, next_ref, edges_ref, visit, True)
+        walk(y_points, x_points, next_ref, first_ref, last_ref, visit, True)
+        for each in sea_edges:
+            each.wait()
+        to_rows(west_ref, 0, west_rim_ref, 8, y_points, rows, 4)
+        to_rows(east_ref, 0, east_rim_ref, 8, y_points, rows + y_points, 4)
+        sum_neighbours(x_points, y_points, grid_ref, (west_rim_ref, east_rim_ref), sum_ref)
         pair_source.wait_send()
         pair_weight.wait_send()
-        for each in sea_edges:
-            each.wait()
         lax.fori_loop(0, n, sent, 0)
         made.wait_recv()
 
@@ -453,17 +467,31 @@
 
 
 def end_kernel(
-    x_points, y_points, state_ref, in_ref, regrid_in_ref, stepped_ref, west_ref, east_ref, table_in_ref, grid_ref,
-    source_hbm, weight_hbm, kappa_hbm, adjacent_hbm, edges_hbm, rate_hbm,
+    x_points, y_points, state_ref, in_ref, made_ref, stepped_ref, west_ref, east_ref, table_in_ref, sum_ref,
+    low_ref, high_ref, share_ref, kappa_hbm, adjacent_hbm, edges_hbm, rate_hbm,
     new_hbm, table_ref,
-    new_ref, source_ref, weight_ref, low_ref, high_ref, share_ref, value_ref, pair_terms_ref, regrid_ref,
-    kappa_ref, adjacent_ref, next_ref, few_ref, west_rim_ref, east_rim_ref, sum_ref, edges_ref, rate_ref,
-    load_sem, store_sem,
+    new_ref, ratio_ref, value_ref, pair_terms_ref, regrid_ref, kappa_ref, adjacent_ref, next_ref, few_ref,
+    every_ref, first_ref, last_ref, rate_ref, load_sem, store_sem,
 ):
     sec = lax.axis_index("sec")
-    load_rate = pltpu.make_async_copy(rate_hbm, rate_ref, load_sem.at[5])
+    levels, rows = state_ref.shape[1], state_ref.shape[2]
+    load_rate = pltpu.make_async_copy(rate_hbm, rate_ref, load_sem.at[0])
+    load_next = pltpu.make_async_copy(adjacent_hbm.at[2], next_ref, load_sem.at[1])
+    load_adjacent = pltpu.make_async_copy(adjacent_hbm, adjacent_ref, load_sem.at[2])
+    load_kappa = pltpu.make_async_copy(kappa_hbm, kappa_ref, load_sem.at[3])
+    load_first = pltpu.make_async_copy(edges_hbm.at[0], first_ref, load_sem.at[4])
+    load_last = pltpu.make_async_copy(edges_hbm.at[1], last_ref, load_sem.at[6])
     load_rate.start()
-    levels, rows = state_ref.shape[1], state_ref.shape[2]
+
+    @pl.when(sec == 1)
+    def _():
+        load_first.start()
+        load_last.start()
+        load_next.start()
+        load_adjacent.start()
+        load_kappa.start()
+
+    load_rate.wait()
 
     def couple(f, here, value, relaxed):
         row = lax.broadcasted_iota(jnp.int32, value.shape, 0)
@@ -471,15 +499,9 @@
 
     @pl.when(sec == 0)
     def _():
-        load_source = pltpu.make_async_copy(source_hbm, source_ref, load_sem.at[0])
-        load_weight = pltpu.make_async_copy(weight_hbm, weight_ref, load_sem.at[1])
-        load_source.start()
-        load_weight.start()
-        load_source.wait()
-        load_weight.wait()
-        load_rate.wait()
-        split_pairs(source_ref, weight_ref, low_ref, high_ref, share_ref)
-        regrid_into(regrid_ref, lambda f: in_ref[1, :, f], low_ref, high_ref, share_ref, pair_terms_ref, value_ref)
+        regrid_into(
+            regrid_ref, lambda f: in_ref[1, :, f], low_ref, high_ref, share_ref, pair_terms_ref, value_ref, ratio_ref
+        )
         stores = [pltpu.make_async_copy(new_ref.at[f], new_hbm.at[f], store_sem.at[f]) for f in range(3)]
         for f in range(3):
             for x in range(x_points):
@@ -515,25 +537,16 @@
 
     @pl.when(sec == 1)
     def _():
-        load_next = pltpu.make_async_copy(adjacent_hbm.at[2], next_ref, load_sem.at[0])
-        load_adjacent = pltpu.make_async_copy(adjacent_hbm, adjacent_ref, load_sem.at[1])
-        load_kappa = pltpu.make_async_copy(kappa_hbm, kappa_ref, load_sem.at[2])
-        load_edges = pltpu.make_async_copy(edges_hbm, edges_ref, load_sem.at[4])
-        load_edges.start()
-        load_next.start()
-        load_adjacent.start()
-        load_kappa.start()
-        to_rows(west_ref, 0, west_rim_ref, 8, y_points, rows, 4)
-        to_rows(east_ref, 0, east_rim_ref, 8, y_points, rows + y_points, 4)
-        sum_neighbours(x_points, y_points, grid_ref, (west_rim_ref, east_rim_ref), sum_ref)
         load_next.wait()
-        load_edges.wait()
-        load_rate.wait()
-
-        def visit(x, base, u, place):
-            table_ref[pl.ds(place, 1), :] = sum_ref[pl.ds(x * y_points + base + u, 1), :]
-
-        walk(y_points, x_points, next_ref, edges_ref, visit, False)
+        load_first.wait()
+        load_last.wait()
+
+        def visit(x, base, places):
+            found = [sum_ref[pl.ds(x * y_points + base + u, 1), :] for u in range(len(places))]
+            for u, place in enumerate(places):
+                table_ref[pl.ds(place, 1), :] = found[u]
+
+        walk(y_points, x_points, next_ref, first_ref, last_ref, visit, False)
         load_adjacent.wait()
         load_kappa.wait()
         part = rows // 4
@@ -551,7 +564,7 @@
             for f in range(3):
                 value = state_ref[f, :, here]
                 swept = value + kappa * (block[f * levels : (f + 1) * levels] - 6.0 * value)
-                couple(f, here, swept, regrid_in_ref[f, pl.ds(c, 1), :])
+                couple(f, here, swept, made_ref[f, pl.ds(c, 1), :])
             named = adjacent_ref[:, here].astype(jnp.float32)
             names = block[24:32]
             off = (names[0:6] != named).astype(jnp.float32)
@@ -567,21 +580,21 @@
 
         @pl.when(jnp.max(wrong) > 0.0)
         def _():
-            to_rows(state_ref, 0, sum_ref, 0, rows, 0, 1)
-            to_rows(west_ref, 0, sum_ref, rows, y_points, rows, 1)
-            to_rows(east_ref, 0, sum_ref, rows + y_points, y_points, rows + y_points, 1)
+            to_rows(state_ref, 0, every_ref, 0, rows, 0, 1)
+            to_rows(west_ref, 0, every_ref, rows, y_points, rows, 1)
+            to_rows(east_ref, 0, every_ref, rows + y_points, y_points, rows + y_points, 1)
 
             def block(c, _):
                 fetch = pltpu.make_async_copy(
-                    adjacent_hbm.at[:, pl.ds(pl.multiple_of(c * LANES, LANES), LANES)], few_ref, load_sem.at[3]
+                    adjacent_hbm.at[:, pl.ds(pl.multiple_of(c * LANES, LANES), LANES)], few_ref, load_sem.at[5]
                 )
                 fetch.start()
                 fetch.wait()
 
                 def cell(i, _):
-                    total = sum_ref[pl.ds(few_ref[0, i], 1), :]
+                    total = every_ref[pl.ds(few_ref[0, i], 1), :]
                     for j in range(1, 6):
-                        total = total + sum_ref[pl.ds(few_ref[j, i], 1), :]
+                        total = total + every_ref[pl.ds(few_ref[j, i], 1), :]
                     table_ref[pl.ds(c * LANES + i, 1), :] = total
                     return 0
 
@@ -619,44 +632,41 @@
     border = jax.ShapeDtypeStruct((3, levels, y_points), f32)
     whole = jax.ShapeDtypeStruct(state.shape, f32)
     table = jax.ShapeDtypeStruct((rows, LANES), f32)
+    index, share = jax.ShapeDtypeStruct((pairs, LANES), i32), jax.ShapeDtypeStruct((pairs, LANES), f32)
+    arriving = jax.ShapeDtypeStruct((2, n, 3, lines, LANES), f32)
     made = jax.ShapeDtypeStruct((3, rows // LANES, LANES), f32)
-    pair_scratch = [
-        pltpu.VMEM((pairs, LANES), i32),
-        pltpu.VMEM((pairs, LANES), f32),
-        pltpu.VMEM((pairs, LANES), i32),
-        pltpu.VMEM((pairs, LANES), i32),
-        pltpu.VMEM((pairs, LANES), f32),
-        pltpu.VMEM((3, pairs, LANES), f32),
-    ]
     dma = pltpu.SemaphoreType.DMA
-    held, incoming, regrid, stepped, west, east, cells, grid = pl.pallas_call(
+    held = pl.pallas_call(
         functools.partial(start_kernel, n, x_points, y_points),
-        out_shape=[
-            whole,
-            jax.ShapeDtypeStruct((2, n, 3, lines, LANES), f32),
-            made,
-            whole,
-            border,
-            border,
-            table,
-            jax.ShapeDtypeStruct(((x_points + 2) * y_points + 16, LANES), f32),
-        ],
+        out_shape=[whole, arriving, made, whole, border, border, table, table, index, index, share],
         in_specs=[HBM] * 8,
-        out_specs=[VMEM] * 8,
+        out_specs=[VMEM] * 11,
         scratch_shapes=[
             pltpu.VMEM((pairs, LANES), i32),
             pltpu.VMEM(atm_metric.shape, f32),
-            *pair_scratch,
+            pltpu.VMEM((pairs, LANES), i32),
+            pltpu.VMEM((pairs, LANES), f32),
+            pltpu.VMEM((pairs, LANES), i32),
+            pltpu.VMEM((pairs, LANES), f32),
+            pltpu.VMEM((pairs, LANES), i32),
+            pltpu.VMEM((pairs, LANES), i32),
+            pltpu.VMEM((pairs, LANES), f32),
+            pltpu.VMEM((3, pairs, LANES), f32),
+            pltpu.VMEM((pairs, LANES), f32),
+            pltpu.VMEM((3 * pairs, 2 * LANES), jnp.bfloat16),
             pltpu.VMEM(made.shape, f32),
             pltpu.VMEM((3 * rows // LANES, LANES), f32),
             pltpu.VMEM((3 * rows // LANES, 2 * LANES), jnp.bfloat16),
-            pltpu.VMEM((3 * pairs, 2 * LANES), jnp.bfloat16),
-            pltpu.VMEM((n, 3, lines, LANES), f32),
+            pltpu.VMEM(arriving.shape[1:], f32),
             pltpu.VMEM((3, levels, 2 * y_points), f32),
+            pltpu.VMEM(((x_points + 2) * y_points + 16, LANES), f32),
+            pltpu.VMEM((y_points + 16, LANES), f32),
+            pltpu.VMEM((y_points + 16, LANES), f32),
             pltpu.SMEM((rows,), i32),
-            pltpu.SMEM(ocean_edges.shape, i32),
+            pltpu.SMEM((y_points,), i32),
+            pltpu.SMEM((y_points,), i32),
             pltpu.SMEM(wave_speed.shape, f32),
-            dma((6,)),
+            dma((9,)),
             dma((n,)),
             dma((2, n)),
             dma((2,)),
@@ -668,39 +678,34 @@
         ],
         compiler_params=pltpu.CompilerParams(collective_id=0, has_side_effects=True, **PARAMS),
         name="start",
-    )(
-        placed, slot_rows, source, weight, metric, adjacent, edges, speed,
-    )
+    )(placed, slot_rows, source, weight, metric, adjacent, edges, speed)
 
     new_state, _ = pl.pallas_call(
         functools.partial(end_kernel, x_points, y_points),
         out_shape=[whole, table],
-        in_specs=[VMEM] * 8 + [HBM] * 6,
+        in_specs=[VMEM] * 11 + [HBM] * 4,
         out_specs=[HBM, VMEM],
         input_output_aliases={6: 1},
         scratch_shapes=[
             pltpu.VMEM(state.shape, f32),
-            *pair_scratch,
+            pltpu.VMEM((pairs, LANES), f32),
+            pltpu.VMEM((3, pairs, LANES), f32),
             pltpu.VMEM((3 * pairs, 2 * LANES), jnp.bfloat16),
-            pltpu.VMEM(made.shape, f32),
+            pltpu.VMEM((3, rows // LANES, LANES), f32),
             pltpu.VMEM((rows // LANES, LANES), f32),
             pltpu.VMEM(ocean_adjacent.shape, i32),
             pltpu.SMEM((rows,), i32),
             pltpu.SMEM((6, LANES), i32),
-            pltpu.VMEM((y_points + 16, LANES), f32),
-            pltpu.VMEM((y_points + 16, LANES), f32),
             pltpu.VMEM((rows + 2 * y_points, LANES), f32),
-            pltpu.SMEM(ocean_edges.shape, i32),
+            pltpu.SMEM((y_points,), i32),
+            pltpu.SMEM((y_points,), i32),
             pltpu.SMEM(couple_rate.shape, f32),
-            dma((6,)),
+            dma((7,)),
             dma((4,)),
         ],
         compiler_params=pltpu.CompilerParams(**PARAMS),
         name="end",
-    )(
-        held, incoming, regrid, stepped, west, east, cells, grid,
-        source, weight, kappa, adjacent, edges, rate,
-    )
+    )(*held, kappa, adjacent, edges, rate)
     return new_state
 
 

time: 30 us -> 27.5 us (0.917)
  Pallas kernels: 29.8 us -> 27.4 us
    pallas_call x1, Pallas kernels: 10.6 us -> 8.65 us  [body(): pl.pallas_call(functools.partial(end_kernel, x_points, y_points), out_sha...]
    pallas_call x1, Pallas kernels: 19.2 us -> 18.7 us  [body(): pl.pallas_call(functools.partial(start_kernel, n, x_points, y_points), ou...]
where the time goes in v2:
time: 27.5 us; the launch traced here: 27.4 us
  Pallas kernels  27.4 us (100%)
    pallas_call x1, Pallas kernels, body(): pl.pallas_call(functools.partial(start_kernel, n, x_points, y_points), ou...  18.7 us
    pallas_call x1, Pallas kernels, body(): pl.pallas_call(functools.partial(end_kernel, x_points, y_points), out_sha...  8.65 us

profile of v2, /device:TPU:1, one launch (start us, length us, event | category | flops | bytes accessed | tf_op | source)
XLA Modules:
  0.0 27.4 jit_solution(16316664299777910659)
XLA Ops:
  0.0 18.7 %start.1 = (f32[3,8,8192]{2,1,0:T(8,128)S(1)}, f32[2,16,3,8,128]{4,3,2,1,0:T(8,128)S(1)}, f32[3,64,128]{2,1,0:T(8,128)S(1)}, f32[3,8,8192]{2,1,0:T(8,128)S(1)}, ...) custom-call(f32[3,8,8192]{2,1,0:T(8,128)} %state_hbm.1, ...), custom_call_target="tpu_custom_call" | custom-call | tf_op jit(solution)/shard_map/start/pallas_call | solution.py:639
  18.8 8.6 %end.1 = (f32[3,8,8192]{2,1,0:T(8,128)}, f32[8192,128]{1,0:T(8,128)S(1)}) custom-call(f32[3,8,8192]{2,1,0:T(8,128)S(1)} %get-tuple-element.17.state_ref, f32[2,16,3,8,128]{4,3,2,1,0:T(8,128)S(1)} %get-tuple-element.18.in_ref, f32[3,64,128]{2,1,0:T(8,128)S(1)} %get-tuple-element.19.made_ref, ...), custom_call_target="tpu_custom_call", output_to_operand_aliasing={{1}: (6, {})} | custom-call | tf_op jit(solution)/shard_map/end/pallas_call | solution.py:683

commit v3 on v2

--- a/solution.py
+++ b/solution.py
@@ -172,18 +172,18 @@
 
 def walk(y_points, x_points, next_ref, first_ref, last_ref, visit, middle):
     def chain(c, _):
-        base = pl.multiple_of(c * 16, 16)
-        places = [first_ref[base + u] for u in range(16)]
+        base = pl.multiple_of(c * 8, 8)
+        places = [first_ref[base + u] for u in range(8)]
         for x in range(x_points - 1):
             if x or not middle:
                 visit(x, base, places)
             if x < x_points - 2:
                 places = [next_ref[place] for place in places]
         if not middle:
-            visit(x_points - 1, base, [last_ref[base + u] for u in range(16)])
+            visit(x_points - 1, base, [last_ref[base + u] for u in range(8)])
         return 0
 
-    lax.fori_loop(0, y_points // 16, chain, 0)
+    lax.fori_loop(0, y_points // 8, chain, 0)
 
 
 def start_kernel(
@@ -243,13 +243,10 @@
     load_state.wait()
     depth, top, rows = state_ref.shape[2] // LANES, state_ref.shape[1] - 1, state_ref.shape[2]
 
-    def column(x, u):
-        return pl.ds(8 + (x + 1) * y_points + u, 1)
-
     def visit(x, base, places):
         found = [table_ref[pl.ds(place, 1), :] for place in places]
         for u in range(len(places)):
-            grid_ref[column(x, base + u), :] = found[u]
+            grid_ref[pl.ds(base + (8 + (x + 1) * y_points + u), 1), :] = found[u]
 
     @pl.when(ocean)
     def _():
@@ -258,12 +255,12 @@
         load_last.wait()
 
         def edge(c, _):
-            base = pl.multiple_of(c * 16, 16)
+            base = pl.multiple_of(c * 8, 8)
             for listed, x in ((first_ref, 0), (last_ref, x_points - 1)):
-                visit(x, base, [listed[base + u] for u in range(16)])
+                visit(x, base, [listed[base + u] for u in range(8)])
             return 0
 
-        lax.fori_loop(0, y_points // 16, edge, 0)
+        lax.fori_loop(0, y_points // 8, edge, 0)
         levels = top + 1
         for k, x in ((0, 0), (1, x_points - 1)):
             for c in range(y_points // LANES):
@@ -300,43 +297,6 @@
     pair_source = remote(source_hbm, sea_source_ref, pair_send.at[0], pair_recv.at[0], (0, dom))
     pair_weight = remote(weight_hbm, sea_weight_ref, pair_send.at[1], pair_recv.at[1], (0, dom))
     made = remote(made_ref, regrid_ref, made_send, made_recv, (1, dom))
-
-    def send(k, _):
-        c = lax.rem(k + dom * chunks // n, chunks)
-        index = row_of(rows_ref, c * CHUNK, CHUNK)
-        values = pick(terms_ref[...], depth, index & (LANES - 1), index >> 7)
-        for f in range(3):
-            for r in range(CHUNK):
-                out_ref[c * peers + r // lines, f, pl.ds(r % lines, 1), :] = values[f][:, r * LANES : (r + 1) * LANES]
-
-        @pl.when(jnp.logical_and(k == 0, atmosphere))
-        def _():
-            pl.semaphore_wait(barrier, n)
-
-        @pl.when(jnp.logical_and(k == 0, ocean))
-        def _():
-            pl.semaphore_wait(barrier, n + 2)
-            pair_source.start()
-            pair_weight.start()
-
-        def ship(j, _):
-            p = c * peers + j
-            here = jnp.logical_and(atmosphere, p == dom)
-
-            @pl.when(here)
-            def _():
-                own_slots().start()
-
-            @pl.when(jnp.logical_not(here))
-            def _():
-                slots(p).start()
-
-            return 0
-
-        lax.fori_loop(0, peers, ship, 0)
-        return 0
-
-    lax.fori_loop(0, chunks, send, 0)
 
     first, last = pl.ds(0, y_points), pl.ds(rows - y_points, y_points)
     rim_first, rim_last = rim_ref.at[:, :, first], rim_ref.at[:, :, pl.ds(y_points, y_points)]
@@ -348,6 +308,45 @@
         remote(rim_last, west_ref, edge_send.at[0], edge_recv.at[0], (1, right)),
         remote(rim_first, east_ref, edge_send.at[1], edge_recv.at[1], (1, left)),
     ]
+
+    def send(k, _):
+        c = lax.rem(k + dom * chunks // n, chunks)
+        index = row_of(rows_ref, c * CHUNK, CHUNK)
+        values = pick(terms_ref[...], depth, index & (LANES - 1), index >> 7)
+        for f in range(3):
+            for r in range(CHUNK):
+                out_ref[c * peers + r // lines, f, pl.ds(r % lines, 1), :] = values[f][:, r * LANES : (r + 1) * LANES]
+
+        @pl.when(jnp.logical_and(k == 0, atmosphere))
+        def _():
+            pl.semaphore_wait(barrier, n)
+
+        @pl.when(jnp.logical_and(k == 0, ocean))
+        def _():
+            pl.semaphore_wait(barrier, n + 2)
+            for each in sea_edges:
+                each.start()
+            pair_source.start()
+            pair_weight.start()
+
+        def ship(j, _):
+            p = c * peers + j
+            here = jnp.logical_and(atmosphere, p == dom)
+
+            @pl.when(here)
+            def _():
+                own_slots().start()
+
+            @pl.when(jnp.logical_not(here))
+            def _():
+                slots(p).start()
+
+            return 0
+
+        lax.fori_loop(0, peers, ship, 0)
+        return 0
+
+    lax.fori_loop(0, chunks, send, 0)
 
     def sent(p, _):
         @pl.when(jnp.logical_not(jnp.logical_and(atmosphere, p == dom)))
@@ -403,22 +402,22 @@
 
     @pl.when(ocean)
     def _():
-        for each in sea_edges:
-            each.start()
         load_next.wait()
         walk(y_points, x_points, next_ref, first_ref, last_ref, visit, True)
+        rims = (west_rim_ref, east_rim_ref)
+        sum_neighbours(x_points, y_points, grid_ref, rims, sum_ref, [range(1, x_points - 1)])
         for each in sea_edges:
             each.wait()
         to_rows(west_ref, 0, west_rim_ref, 8, y_points, rows, 4)
         to_rows(east_ref, 0, east_rim_ref, 8, y_points, rows + y_points, 4)
-        sum_neighbours(x_points, y_points, grid_ref, (west_rim_ref, east_rim_ref), sum_ref)
+        sum_neighbours(x_points, y_points, grid_ref, rims, sum_ref, [range(1), range(x_points - 1, x_points)])
         pair_source.wait_send()
         pair_weight.wait_send()
         lax.fori_loop(0, n, sent, 0)
         made.wait_recv()
 
 
-def sum_neighbours(x_points, y_points, grid_ref, rims, sum_ref):
+def sum_neighbours(x_points, y_points, grid_ref, rims, sum_ref, spans):
     lane = lax.broadcasted_iota(jnp.int32, (8, LANES), 1)
     row = lax.broadcasted_iota(jnp.int32, (8, LANES), 0)
 
@@ -434,25 +433,26 @@
 
     def read(x, at, shift):
         if 0 <= x < x_points:
-            return grid_ref[pl.ds(8 + (x + 1) * y_points + at + shift, 8), :]
-        return rims[0 if x < 0 else 1][pl.ds(8 + at + shift, 8), :]
+            return grid_ref[pl.ds(at + (8 + (x + 1) * y_points + shift), 8), :]
+        return rims[0 if x < 0 else 1][pl.ds(at + (8 + shift), 8), :]
 
     def inner(c, _):
         at = c * 8
-        joined = {}
-        for x in range(-1, x_points + 1):
-            tilt = -1 if x % 2 else 1
-            joined[x] = read(x, at, 0) * same + read(x, at, tilt) * tilted
-            if x > 0:
-                upright = read(x - 1, at, 1) * above + read(x - 1, at, -1) * below
-                total = upright + joined[x] * east + joined[x - 2] * west
-                sum_ref[pl.ds(pl.multiple_of((x - 1) * y_points + at, 8), 8), :] = total
+        for span in spans:
+            joined, upright = {}, {}
+            for x in range(span.start - 1, span.stop + 1):
+                middle, up, down = read(x, at, 0), read(x, at, 1), read(x, at, -1)
+                joined[x] = middle * same + (down if x % 2 else up) * tilted
+                upright[x] = up * above + down * below
+                if x > span.start:
+                    total = upright[x - 1] + joined[x] * east + joined[x - 2] * west
+                    sum_ref[pl.ds(pl.multiple_of(at + (x - 1) * y_points, 8), 8), :] = total
         return 0
 
     lax.fori_loop(1, y_points // 8 - 1, inner, 0)
 
     for at, gone, missing in ((0, row == 0, -1), (y_points - 8, row == 7, 1)):
-        for x in range(x_points):
+        for x in [x for span in spans for x in span]:
             own = read(x, at, 0)
             tilt = 1 if x % 2 else -1
 
@@ -542,7 +542,7 @@
         load_last.wait()
 
         def visit(x, base, places):
-            found = [sum_ref[pl.ds(x * y_points + base + u, 1), :] for u in range(len(places))]
+            found = [sum_ref[pl.ds(base + (x * y_points + u), 1), :] for u in range(len(places))]
             for u, place in enumerate(places):
                 table_ref[pl.ds(place, 1), :] = found[u]
 

time: 27.5 us -> 26.4 us (0.960)
  Pallas kernels: 27.4 us -> 26.1 us
    pallas_call x1, Pallas kernels: 18.7 us -> 17.6 us  [body(): pl.pallas_call(functools.partial(start_kernel, n, x_points, y_points), ou...]
where the time goes in v3:
time: 26.4 us; the launch traced here: 26.1 us
  Pallas kernels  26.1 us (99%)
    pallas_call x1, Pallas kernels, body(): pl.pallas_call(functools.partial(start_kernel, n, x_points, y_points), ou...  17.6 us
    pallas_call x1, Pallas kernels, body(): pl.pallas_call(functools.partial(end_kernel, x_points, y_points), out_sha...  8.55 us

profile of v3, /device:TPU:1, one launch (start us, length us, event | category | flops | bytes accessed | tf_op | source)
XLA Modules:
  0.0 26.1 jit_solution(8373956225397175455)
XLA Ops:
  0.0 17.6 %start.1 = (f32[3,8,8192]{2,1,0:T(8,128)S(1)}, f32[2,16,3,8,128]{4,3,2,1,0:T(8,128)S(1)}, f32[3,64,128]{2,1,0:T(8,128)S(1)}, f32[3,8,8192]{2,1,0:T(8,128)S(1)}, ...) custom-call(f32[3,8,8192]{2,1,0:T(8,128)} %state_hbm.1, ...), custom_call_target="tpu_custom_call" | custom-call | tf_op jit(solution)/shard_map/start/pallas_call | solution.py:639
  17.6 8.5 %end.1 = (f32[3,8,8192]{2,1,0:T(8,128)}, f32[8192,128]{1,0:T(8,128)S(1)}) custom-call(f32[3,8,8192]{2,1,0:T(8,128)S(1)} %get-tuple-element.17.state_ref, f32[2,16,3,8,128]{4,3,2,1,0:T(8,128)S(1)} %get-tuple-element.18.in_ref, f32[3,64,128]{2,1,0:T(8,128)S(1)} %get-tuple-element.19.made_ref, ...), custom_call_target="tpu_custom_call", output_to_operand_aliasing={{1}: (6, {})} | custom-call | tf_op jit(solution)/shard_map/end/pallas_call | solution.py:683

commit v4 on v3

--- a/solution.py
+++ b/solution.py
@@ -12,7 +12,7 @@
 VMEM = pl.BlockSpec(memory_space=pltpu.VMEM)
 SMEM = pl.BlockSpec(memory_space=pltpu.SMEM)
 HBM = pl.BlockSpec(memory_space=pltpu.HBM)
-PARAMS = dict(vmem_limit_bytes=24 << 20)
+PARAMS = dict(vmem_limit_bytes=36 << 20)
 
 
 def gll_derivative():
@@ -137,14 +137,14 @@
         terms_ref[f * depth : (f + 1) * depth, :] = two_terms(arrived(f).reshape(depth, LANES))
 
     def step(c, _):
-        low, high = row_of(low_ref, c * CHUNK, CHUNK), row_of(high_ref, c * CHUNK, CHUNK)
+        low, high = row_of(low_ref, c * (2 * CHUNK), (2 * CHUNK)), row_of(high_ref, c * (2 * CHUNK), (2 * CHUNK))
         values = pick(terms_ref[...], depth, low, high)
         for f in range(3):
-            for r in range(CHUNK):
-                value_ref[f, pl.ds(c * CHUNK + r, 1), :] = values[f][:, r * LANES : (r + 1) * LANES]
+            for r in range((2 * CHUNK)):
+                value_ref[f, pl.ds(c * (2 * CHUNK) + r, 1), :] = values[f][:, r * LANES : (r + 1) * LANES]
         return 0
 
-    lax.fori_loop(0, depth // CHUNK, step, 0)
+    lax.fori_loop(0, depth // (2 * CHUNK), step, 0)
     share = share_ref[...]
     whole = share + pltpu.roll(share, LANES // 2, 1)
     first = lax.broadcasted_iota(jnp.int32, (depth // 2, LANES), 1) < LANES // 2
@@ -250,7 +250,7 @@
 
     @pl.when(ocean)
     def _():
-        to_rows(state_ref, 0, table_ref, 0, rows, 0, 8)
+        to_rows(state_ref, 0, table_ref, 0, rows, 0, 16)
         load_first.wait()
         load_last.wait()
 
@@ -573,7 +573,7 @@
         wrong = jnp.zeros((1, LANES), jnp.float32)
         for k in range(4):
             blocks = part // LANES
-            wrong = lax.fori_loop(k * blocks, (k + 1) * blocks, finish, wrong, unroll=8)
+            wrong = lax.fori_loop(k * blocks, (k + 1) * blocks, finish, wrong, unroll=16)
             stores[k].start()
         for each in stores:
             each.wait()

time: 26.4 us -> 25.9 us (0.981)
  the two profiles are of different devices: /device:TPU:1 before, /device:TPU:15 now
where the time goes in v4:
time: 25.9 us; the launch traced here: 25.8 us
  Pallas kernels  25.8 us (100%)
    pallas_call x1, Pallas kernels, body(): pl.pallas_call(functools.partial(start_kernel, n, x_points, y_points), ou...  17.6 us
    pallas_call x1, Pallas kernels, body(): pl.pallas_call(functools.partial(end_kernel, x_points, y_points), out_sha...  8.17 us

profile of v4, /device:TPU:15, one launch (start us, length us, event | category | flops | bytes accessed | tf_op | source)
XLA Modules:
  0.0 25.8 jit_solution(6368056553253229409)
XLA Ops:
  0.0 17.6 %start.1 = (f32[3,8,8192]{2,1,0:T(8,128)S(1)}, f32[2,16,3,8,128]{4,3,2,1,0:T(8,128)S(1)}, f32[3,64,128]{2,1,0:T(8,128)S(1)}, f32[3,8,8192]{2,1,0:T(8,128)S(1)}, ...) custom-call(f32[3,8,8192]{2,1,0:T(8,128)} %state_hbm.1, ...), custom_call_target="tpu_custom_call" | custom-call | tf_op jit(solution)/shard_map/start/pallas_call | solution.py:639
  17.6 8.2 %end.1 = (f32[3,8,8192]{2,1,0:T(8,128)}, f32[8192,128]{1,0:T(8,128)S(1)}) custom-call(f32[3,8,8192]{2,1,0:T(8,128)S(1)} %get-tuple-element.17.state_ref, f32[2,16,3,8,128]{4,3,2,1,0:T(8,128)S(1)} %get-tuple-element.18.in_ref, f32[3,64,128]{2,1,0:T(8,128)S(1)} %get-tuple-element.19.made_ref, ...), custom_call_target="tpu_custom_call", output_to_operand_aliasing={{1}: (6, {})} | custom-call | tf_op jit(solution)/shard_map/end/pallas_call | solution.py:683
